TPU v7x, 32 devices: a whole 2x2x4 slice. The times are simulated.
32 devices in a mesh: section: 2 (over core), mesh: 16 (over z, y, x).
Axes of the slice: x: 2, y: 2, z: 4, core: 2. Of those that a mesh axis runs over, the one named last changes fastest.
Arguments:
- saved_inputs: bfloat16 [2, 3, 4096, 1024], P('section', None, 'mesh'), may hold values from -8 to 8
- w_query: bfloat16 [2, 1024, 1024], P('section'), may hold values from -6 to 6
- w_key: bfloat16 [2, 1024, 1024], P('section'), may hold values from -6 to 6
- w_value: bfloat16 [2, 1024, 1024], P('section'), may hold values from -0.1875 to 0.1875
- w_out: bfloat16 [2, 1024, 1024], P('section'), may hold values from -0.1875 to 0.1875
- pending: bfloat16 [2, 4096, 1024], P('section', 'mesh'), may hold values from -6 to 6
- top_grads: bfloat16 [1, 4096, 1024], P(None, 'mesh'), may hold values from -6 to 6
- key_blocks: int32 [32, 2], P('mesh'), may hold values from -1 to 31, as said below
- counts: int32 [32], replicated, may hold values from 64 to 128, as said below
- plan: int32 [2, 2], replicated, may hold values from 0 to 2
Outputs:
- layer_grads: float32 [2, 1024, 4, 1024], P('section', 'mesh')
- input_grads: bfloat16 [2, 2, 4096, 1024], P(None, 'section', 'mesh')
Inputs may be any that keep to these rules, and one draw needn't show every extreme that they name: `key_blocks`: entry j of block b is -1 (nothing read) or the block (b + o_j) modulo 32, with o = (1, -1). `counts`: the padding nodes of a block are its last ones.
All inputs are finite; a program needn't handle non-finite values.
Results may differ from a plain program's by a relative error of at most 0.03.
The roundings to bfloat16 on the way count: a program that leaves them out, or rounds other values in their place, can miss the bound.
Values may be sent and summed in bfloat16 or wider, within the bound.
A program may use at most 128 MiB of HBM per device.

v0:
```python
import math

import jax
import jax.numpy as jnp
from jax import lax
from jax.sharding import PartitionSpec as P

HEADS = 8
BLOCK = 128


OFFSETS = (1, -1)
EPSILON = 1e-06


def from_behind(value, axis, steps):
    count = lax.axis_size(axis)
    pairs = [(source, (source + steps) % count) for source in range(count)]
    return lax.ppermute(value, axis, pairs)


def shifted(x, axis, by):
    size = lax.axis_size(axis)
    pairs = [(i, i + by) for i in range(size) if 0 <= i + by < size]
    return lax.ppermute(x, axis, pairs)


def right_dot(left, right):
    return lax.dot_general(
        left, right, (((1,), (1,)), ((), ())), preferred_element_type=jnp.float32
    )


def left_dot(left, right):
    return lax.dot_general(
        left, right, (((0,), (0,)), ((), ())), preferred_element_type=jnp.float32
    )


def weight_rows(terms, row_count):
    normed, grad_joined, attended, upstream = terms
    features = upstream.shape[1]
    projected = left_dot(normed, grad_joined).reshape(row_count, 3, features)
    return jnp.concatenate([projected, left_dot(attended, upstream)[:, None]], axis=1)


def per_device(
    saved_inputs, w_query, w_key, w_value, w_out, pending, top_grads, key_blocks, counts, plan
):
    sections = lax.axis_size("section")
    section_here = lax.axis_index("section")
    part_count = lax.axis_size("mesh")
    part_here = lax.axis_index("mesh")
    rows_here = pending.shape[1]
    features = pending.shape[2]
    block_rows = BLOCK
    blocks_here = rows_here // block_rows
    head_dim = features // HEADS
    tick_count = plan.shape[0]
    score_scale = 1.0 / math.sqrt(head_dim)
    slot_count = 1 + len(OFFSETS)
    query_weight = w_query[0]
    key_weight = w_key[0]
    value_weight = w_value[0]
    out_weight = w_out[0]
    positions = jnp.arange(block_rows)
    block_ids = jnp.arange(counts.shape[0])
    global_ids = part_here * blocks_here + jnp.arange(blocks_here)
    own_count = jnp.sum(
        jnp.where(block_ids[None, :] == global_ids[:, None], counts[None, :], 0), axis=1
    )
    listed_counts = jnp.sum(
        jnp.where(block_ids[None, None, :] == key_blocks[:, :, None], counts[None, None, :], 0),
        axis=2,
    )
    own_valid = positions[None, :] < own_count[:, None]
    listed_valid = positions[None, None, :] < listed_counts[:, :, None]
    key_valid = jnp.concatenate([own_valid[:, None, :], listed_valid], axis=1).reshape(
        blocks_here, slot_count * block_rows
    )
    member_ids = jnp.sum(jnp.where(jnp.arange(sections)[None, :] == section_here, plan, 0), axis=1)
    slot_offsets = (0,) + OFFSETS
    upstream = pending[0]
    outgoing = []
    layer_total = None
    for tick_index in range(tick_count):
        x_in = lax.dynamic_index_in_dim(saved_inputs[0], member_ids[tick_index], 0, keepdims=False)
        x_float = x_in.astype(jnp.float32)
        inv_rms = lax.rsqrt(jnp.mean(x_float * x_float, axis=-1, keepdims=True) + EPSILON)
        normed_float = x_float * inv_rms
        normed = normed_float.astype(jnp.bfloat16)
        queries = jnp.dot(normed, query_weight, preferred_element_type=jnp.float32).astype(
            jnp.bfloat16
        )
        key_rows = jnp.dot(normed, key_weight, preferred_element_type=jnp.float32).astype(
            jnp.bfloat16
        )
        value_rows = jnp.dot(normed, value_weight, preferred_element_type=jnp.float32).astype(
            jnp.bfloat16
        )
        own_pair = jnp.stack([key_rows, value_rows])
        edge_pairs = []
        for direction in (1, -1):
            edge_rows = (
                own_pair[:, rows_here - block_rows :]
                if direction == 1
                else own_pair[:, :block_rows]
            )
            edge_pairs.append(from_behind(edge_rows, "mesh", direction))
        extended = jnp.concatenate([edge_pairs[0], own_pair, edge_pairs[1]], axis=1)
        ext_blocks = extended.reshape(2, blocks_here + 2, block_rows, features)
        chosen = jnp.stack(
            [ext_blocks[:, 1 + offset : 1 + offset + blocks_here] for offset in slot_offsets],
            axis=2,
        )
        key_heads = chosen[0].reshape(blocks_here, slot_count * block_rows, HEADS, head_dim)
        value_heads = chosen[1].reshape(blocks_here, slot_count * block_rows, HEADS, head_dim)
        query_heads = queries.reshape(blocks_here, block_rows, HEADS, head_dim)
        scores = (
            jnp.einsum(
                "bqhd,bkhd->bhqk", query_heads, key_heads, preferred_element_type=jnp.float32
            )
            * score_scale
        )
        scores = jnp.where(key_valid[:, None, None, :], scores, -jnp.inf)
        peak = jnp.max(scores, axis=-1, keepdims=True)
        raised = jnp.exp(scores - peak)
        probs = raised / jnp.sum(raised, axis=-1, keepdims=True)
        probs_bf = probs.astype(jnp.bfloat16)
        attended = (
            jnp.einsum("bhqk,bkhd->bqhd", probs_bf, value_heads, preferred_element_type=jnp.float32)
            .reshape(rows_here, features)
            .astype(jnp.bfloat16)
        )
        grad_attended = right_dot(upstream, out_weight).astype(jnp.bfloat16)
        grad_heads = grad_attended.reshape(blocks_here, block_rows, HEADS, head_dim)
        grad_probs = jnp.einsum(
            "bqhd,bkhd->bhqk", grad_heads, value_heads, preferred_element_type=jnp.float32
        )
        grad_scores = (
            probs * (grad_probs - jnp.sum(probs * grad_probs, axis=-1, keepdims=True)) * score_scale
        )
        scores_bf = grad_scores.astype(jnp.bfloat16)
        grad_query = (
            jnp.einsum("bhqk,bkhd->bqhd", scores_bf, key_heads, preferred_element_type=jnp.float32)
            .reshape(rows_here, features)
            .astype(jnp.bfloat16)
        )
        key_terms = jnp.einsum(
            "bhqk,bqhd->bkhd", scores_bf, query_heads, preferred_element_type=jnp.float32
        ).reshape(blocks_here, slot_count, block_rows, features)
        value_terms = jnp.einsum(
            "bhqk,bqhd->bkhd", probs_bf, grad_heads, preferred_element_type=jnp.float32
        ).reshape(blocks_here, slot_count, block_rows, features)
        own_list = []
        before_list = []
        after_list = []
        for terms_now in (key_terms, value_terms):
            zero_block = jnp.zeros_like(terms_now[:1, 0])
            own_now = (
                terms_now[:, 0]
                + jnp.concatenate([zero_block, terms_now[:-1, 1]], axis=0)
                + jnp.concatenate([terms_now[1:, 2], zero_block], axis=0)
            )
            own_list.append(own_now)
            before_list.append(terms_now[0, 2])
            after_list.append(terms_now[blocks_here - 1, 1])
        own_terms = jnp.stack(own_list)
        for direction in (-1, 1):
            edge_terms = jnp.stack(before_list) if direction == -1 else jnp.stack(after_list)
            target_index = blocks_here - 1 if direction == -1 else 0
            returned = from_behind(edge_terms.astype(jnp.bfloat16), "mesh", direction)
            own_terms = own_terms.at[:, target_index].add(returned.astype(jnp.float32))
        grad_key = own_terms[0].reshape(rows_here, features).astype(jnp.bfloat16)
        grad_value = own_terms[1].reshape(rows_here, features).astype(jnp.bfloat16)
        grad_normed = (
            right_dot(grad_query, query_weight)
            + right_dot(grad_key, key_weight)
            + right_dot(grad_value, value_weight)
        )
        grad_input = inv_rms * (
            grad_normed
            - normed_float * jnp.mean(grad_normed * normed_float, axis=-1, keepdims=True)
        )
        grad_x = (upstream.astype(jnp.float32) + grad_input).astype(jnp.bfloat16)
        outgoing.append(grad_x)
        grad_joined = jnp.concatenate([grad_query, grad_key, grad_value], axis=1)
        terms = (normed, grad_joined, attended, upstream)

        def tick_rows(first_row, row_count, terms=terms):
            return weight_rows(terms, row_count)

        tick_sum = lax.psum_scatter(
            tick_rows(jnp.int32(0), features // part_count * lax.axis_size("mesh")).astype(
                jnp.bfloat16
            ),
            "mesh",
            scatter_dimension=0,
            tiled=True,
        ).astype(jnp.float32)
        layer_total = tick_sum if layer_total is None else layer_total + tick_sum
        if tick_index + 1 < tick_count:
            passed = shifted(grad_x, "section", -1)
            upstream = jnp.where(section_here == sections - 1, top_grads[tick_index], passed)
    return (layer_total[None], jnp.stack(outgoing)[:, None])


def solution(mesh):
    in_specs = (
        P("section", None, "mesh", None),
        P("section", None, None),
        P("section", None, None),
        P("section", None, None),
        P("section", None, None),
        P("section", "mesh", None),
        P(None, "mesh", None),
        P("mesh", None),
        P(),
        P(),
    )
    out_specs = (P("section", "mesh", None, None), P(None, "section", "mesh", None))
    return jax.shard_map(
        per_device, mesh=mesh, in_specs=in_specs, out_specs=out_specs, check_vma=False
    )
```

profile of v0, /device:TPU:0, one launch (start us, length us, event | category | flops | bytes accessed | tf_op | source)
XLA Modules:
  0.0 592.7 jit_solution(15003034801554418081)
XLA Ops:
  14.1 2.5 fusion.139
  16.7 2.0 fusion.145
  19.9 2.9 collective-permute-start
  22.8 4.0 collective-permute-start.1
  27.5 2.6 fusion.133
  31.3 2.3 fusion.127
  34.1 11.5 %collective-permute-done = bf16[2,128,1024]{2,1,0:T(8,128)(2,1)} collective-permute-done((bf16[2,128,1024]{2,1,0:T(8,128)(2,1)}, bf16[2,128,1024]{2,1,0:T(8,128)(2,1)}, u32[]{:S(2)}, u32[]{:S(2)}) %collective-permute-start) | collective-permute-done | bytes 524320 | tf_op jit(solution)/shard_map/ppermute | solution.py:19
  53.1 3.3 copy.98
  56.4 3.0 copy.128
  59.4 2.8 copy.88
  62.3 3.8 fusion.238
  66.0 4.1 fusion.236
  70.2 4.2 fusion.148
  74.4 2.3 convolution_bitcast_fusion.1
  76.7 17.9 %fusion.55 = f32[2,384,8,128]{1,3,2,0:T(8,128)} fusion(bf16[2,128,8,128]{1,3,2,0:T(8,128)(2,1)S(1)} %copy-done.35, f32[2,8,128,384]{3,2,1,0:T(8,128)} %fusion.238, f32[2,8,128,384]{3,2,1,0:T(8,128)} %get-tuple-element.95, f32[2,8,128]{2,1,0:T(8,128)S(1)} %get-tuple-element.94), kind=kOutput, calls=%fused_computation.65 | convolution fusion | flops 206834048 | bytes 9969664 | tf_op jit(solution)/shard_map/bhqk,bqhd->bkhd/dot_general | solution.py:149
  94.5 3.6 copy.91
  98.1 4.6 reshape.346
  102.7 2.3 slice_bitcast_fusion.17
  105.0 3.3 convert.60
  108.3 3.6 copy.94
  111.9 4.6 reshape.347
  117.7 2.1 convert.61
  121.9 3.4 collective-permute-start.2
  126.4 2.9 fusion.180
  129.3 17.2 %fusion.118 = bf16[2,128,8,128]{1,3,2,0:T(8,128)(2,1)} fusion(bf16[2,384,8,128]{1,3,2,0:T(8,128)(2,1)} %copy.88, f32[2,8,128,384]{3,2,1,0:T(8,128)} %fusion.238, f32[2,8,128,384]{3,2,1,0:T(8,128)} %get-tuple-element.95, f32[2,8,128]{2,1,0:T(8,128)S(1)} %get-tuple-element.94), kind=kOutput, calls=%fused_computation.110 | convolution fusion | flops 207096192 | bytes 8396800 | tf_op jit(solution)/shard_map/bhqk,bkhd->bqhd/dot_general | solution.py:145
  146.5 2.7 pad_maximum_fusion.4
  149.2 2.1 copy.89
  151.3 2.1 copy.99
  154.7 3.3 convert_bitcast_fusion.1
  162.8 2.6 copy.96
  165.3 6.4 %convolution_convert_fusion.1 = bf16[1024,3,1024]{2,0,1:T(8,128)(2,1)} fusion(bf16[3,1024,256]{2,1,0:T(8,128)(2,1)} %bitcast.416, f32[256]{0:T(256)S(1)} %add_rsqrt_fusion.1, bf16[1,3,256,1024]{3,2,1,0:T(8,128)(2,1)} %param.18, s32[]{:T(128)S(6)} %select_n.35), kind=kOutput, calls=%fused_computation.7 | convolution fusion | flops 1614544896 | bytes 8389636 | tf_op jit(solution)/shard_map/dot_general | solution.py:35
  171.8 6.8 %pad_maximum_fusion = bf16[1024,4,1024]{2,0,1:T(8,128)(2,1)} fusion(bf16[1024,1,1024]{2,0,1:T(8,128)(2,1)S(1)} %copy-done.11, bf16[1024,3,1024]{2,0,1:T(8,128)(2,1)} %convolution_convert_fusion.1), kind=kLoop, calls=%fused_computation.4 | loop fusion | flops 4194304 | bytes 16777216 | tf_op jit(solution)/shard_map/concatenate | solution.py:44
  178.6 2.5 fusion.136
  181.2 2.0 fusion.142
  185.3 4.9 collective-permute-start.5
  190.2 2.5 fusion.130
  194.0 40.0 %collective-permute-done.4 = bf16[2,128,1024]{2,1,0:T(8,128)(2,1)} collective-permute-done((bf16[2,128,1024]{2,1,0:T(8,128)(2,1)}, bf16[2,128,1024]{2,1,0:T(8,128)(2,1)}, u32[]{:S(2)}, u32[]{:S(2)}) %collective-permute-start.4) | collective-permute-done | bytes 524320 | tf_op jit(solution)/shard_map/ppermute | solution.py:19
  239.7 2.9 copy.106
  242.6 3.0 copy.138
  245.6 2.9 copy.116
  248.5 3.3 fusion.18
  251.8 4.5 fusion.237
  256.3 2.5 fusion.26
  263.8 2.1 copy.117
  267.1 2.5 fusion.124
  270.1 4.3 convolution_bitcast_fusion
  274.4 3.6 copy.112
  278.0 4.6 reshape.354
  282.5 3.7 fusion.239
  286.3 17.8 %fusion.52 = f32[2,384,8,128]{1,3,2,0:T(8,128)} fusion(bf16[2,128,8,128]{1,3,2,0:T(8,128)(2,1)S(1)} %copy-done.34, f32[2,8,128,384]{3,2,1,0:T(8,128)} %fusion.239, f32[2,8,128,384]{3,2,1,0:T(8,128)} %get-tuple-element.99, f32[2,8,128]{2,1,0:T(8,128)S(1)} %get-tuple-element.98), kind=kOutput, calls=%fused_computation.64 | convolution fusion | flops 206834048 | bytes 9969664 | tf_op jit(solution)/shard_map/bhqk,bqhd->bkhd/dot_general | solution.py:149
  304.0 3.6 copy.109
  307.6 4.5 reshape.353
  312.1 2.3 convert.66
  316.2 3.8 collective-permute-start.7
  322.3 17.2 %fusion.121 = bf16[2,128,8,128]{1,3,2,0:T(8,128)(2,1)} fusion(bf16[2,384,8,128]{1,3,2,0:T(8,128)(2,1)} %copy.106, f32[2,8,128,384]{3,2,1,0:T(8,128)} %fusion.239, f32[2,8,128,384]{3,2,1,0:T(8,128)} %get-tuple-element.99, f32[2,8,128]{2,1,0:T(8,128)S(1)} %get-tuple-element.98), kind=kOutput, calls=%fused_computation.111 | convolution fusion | flops 207096192 | bytes 8396800 | tf_op jit(solution)/shard_map/bhqk,bkhd->bqhd/dot_general | solution.py:145
  343.7 2.1 copy.107
  347.1 3.4 convert_bitcast_fusion
  351.7 13.1 %collective-permute-done.8 = bf16[2,128,1024]{2,1,0:T(8,128)(2,1)} collective-permute-done((bf16[2,128,1024]{2,1,0:T(8,128)(2,1)}, bf16[2,128,1024]{2,1,0:T(8,128)(2,1)}, u32[]{:S(2)}, u32[]{:S(2)}) %collective-permute-start.8) | collective-permute-done | bytes 524320 | tf_op jit(solution)/shard_map/ppermute | solution.py:19
  368.4 2.6 copy.114
  371.0 6.4 %convolution_convert_fusion = bf16[1024,3,1024]{2,0,1:T(8,128)(2,1)} fusion(bf16[3,1024,256]{2,1,0:T(8,128)(2,1)} %bitcast.417, f32[256]{0:T(256)S(1)} %add_rsqrt_fusion, bf16[1,3,256,1024]{3,2,1,0:T(8,128)(2,1)} %param.18, s32[]{:T(128)S(6)} %select_n.39), kind=kOutput, calls=%fused_computation.6 | convolution fusion | flops 1614544896 | bytes 8389636 | tf_op jit(solution)/shard_map/dot_general | solution.py:35
  377.3 6.8 %pad_maximum_fusion.1 = bf16[1024,4,1024]{2,0,1:T(8,128)(2,1)} fusion(bf16[1024,1,1024]{2,0,1:T(8,128)(2,1)S(1)} %copy-done.12, bf16[1024,3,1024]{2,0,1:T(8,128)(2,1)} %convolution_convert_fusion), kind=kLoop, calls=%fused_computation.5 | loop fusion | flops 4194304 | bytes 16777216 | tf_op jit(solution)/shard_map/concatenate | solution.py:44
  385.1 2.5 fusion.16
  392.2 8.1 %reduce-scatter.3.cloned.1.call-done = bf16[64,4,1024]{2,0,1:T(8,128)(2,1)} async-done(((bf16[1024,4,1024]{2,0,1:T(8,128)(2,1)}), bf16[64,4,1024]{2,0,1:T(8,128)(2,1)}) %reduce-scatter.3.cloned.1.call-update) | async-done | bytes 524304 | tf_op jit(solution)/shard_map/reduce_scatter | solution.py:193
  400.2 182.5 %reduce-scatter.5.cloned.1.call-done = bf16[64,4,1024]{2,0,1:T(8,128)(2,1)} async-done(((bf16[1024,4,1024]{2,0,1:T(8,128)(2,1)}), bf16[64,4,1024]{2,0,1:T(8,128)(2,1)}) %reduce-scatter.5.cloned.1.call-update) | async-done | bytes 524304 | tf_op jit(solution)/shard_map/reduce_scatter | solution.py:193
  (163 shorter events, 62.7 us)
Async XLA Ops:
  7.2 9.5 %copy-start = (bf16[1,1024,1024]{2,1,0:T(8,128)(2,1)S(1)}, bf16[1,1024,1024]{2,1,0:T(8,128)(2,1)}, u32[]{:S(2)}) copy-start(bf16[1,1024,1024]{2,1,0:T(8,128)(2,1)} %param.20) | copy-start | bytes 6291460
  7.2 393.1 %reduce-scatter.3.cloned.1.call-start = ((), (), s32[]{:S(2)}) async-start(), calls=%async_computation.2 | async-start | bytes 8912896 | tf_op jit(solution)/shard_map/reduce_scatter | solution.py:193
  16.7 3.2 copy-start.29
  16.7 10.2 %copy-start.37 = (s32[32]{0:T(128)S(1)}, s32[32]{0:T(128)}, u32[]{:S(2)}) copy-start(s32[32]{0:T(128)} %param.26) | copy-start | bytes 388
  16.7 10.4 %copy-start.36 = (s32[2,2]{1,0:T(2,128)S(1)}, s32[2,2]{1,0:T(2,128)}, u32[]{:S(2)}) copy-start(s32[2,2]{1,0:T(2,128)} %param.25) | copy-start | bytes 52
  18.7 1.2 copy-start.30
  19.9 25.7 %collective-permute-start = (bf16[2,128,1024]{2,1,0:T(8,128)(2,1)}, bf16[2,128,1024]{2,1,0:T(8,128)(2,1)}, u32[]{:S(2)}, u32[]{:S(2)}) collective-permute-start(bf16[2,128,1024]{2,1,0:T(8,128)(2,1)} %get-tuple-element.90), channel_id=1, source_target_pairs={{0,1},{1,2},{2,3},{3,4},{4,5},{5,6},{6,7},{7,8},{8,9},{9,10},{10,1... | collective-permute-start | bytes 1572872 | tf_op jit(solution)/shard_map/ppermute | solution.py:19
  22.8 24.7 %collective-permute-start.1 = (bf16[2,128,1024]{2,1,0:T(8,128)(2,1)}, bf16[2,128,1024]{2,1,0:T(8,128)(2,1)}, u32[]{:S(2)}, u32[]{:S(2)}) collective-permute-start(bf16[2,128,1024]{2,1,0:T(8,128)(2,1)} %get-tuple-element.91), channel_id=1, source_target_pairs={{0,15},{1,0},{2,1},{3,2},{4,3},{5,4},{6,5},{7,6},{8,7},{9,8},{10,9... | collective-permute-start | bytes 1572872 | tf_op jit(solution)/shard_map/ppermute | solution.py:19
  27.4 3.8 copy-start.23
  62.3 3.8 copy-start.35
  70.2 4.2 copy-start.39
  119.9 6.5 %copy-start.27 = (f32[1,128,1024]{2,1,0:T(8,128)S(1)}, f32[1,128,1024]{2,1,0:T(8,128)}, u32[]{:S(2)}) copy-start(f32[1,128,1024]{2,1,0:T(8,128)} %get-tuple-element.64) | copy-start | bytes 1572868
  119.9 6.5 %copy-start.28 = (f32[1,128,1024]{2,1,0:T(8,128)S(1)}, f32[1,128,1024]{2,1,0:T(8,128)}, u32[]{:S(2)}) copy-start(f32[1,128,1024]{2,1,0:T(8,128)} %get-tuple-element.65) | copy-start | bytes 1572868
  121.9 36.1 %collective-permute-start.2 = (bf16[2,128,1024]{2,1,0:T(8,128)(2,1)}, bf16[2,128,1024]{2,1,0:T(8,128)(2,1)}, u32[]{:S(2)}, u32[]{:S(2)}) collective-permute-start(bf16[2,128,1024]{2,1,0:T(8,128)(2,1)} %pad_maximum_fusion.10), channel_id=1, source_target_pairs={{0,15},{1,0},{2,1},{3,2},{4,3},{5,4},{6,5},{7,6},{8,7},{9,8},{10,9... | collective-permute-start | bytes 1572872 | tf_op jit(solution)/shard_map/ppermute | solution.py:19
  126.2 33.0 %collective-permute-start.3 = (bf16[2,128,1024]{2,1,0:T(8,128)(2,1)}, bf16[2,128,1024]{2,1,0:T(8,128)(2,1)}, u32[]{:S(2)}, u32[]{:S(2)}) collective-permute-start(bf16[2,128,1024]{2,1,0:T(8,128)(2,1)} %pad_maximum_fusion.11), channel_id=1, source_target_pairs={{0,1},{1,2},{2,3},{3,4},{4,5},{5,6},{6,7},{7,8},{8,9},{9,10},{10,1... | collective-permute-start | bytes 1572872 | tf_op jit(solution)/shard_map/ppermute | solution.py:19
  153.4 4.6 copy-start.7
  153.4 4.6 copy-start.9
  160.7 0.8 copy-start.18
  165.3 6.4 %copy-start.11 = (bf16[1024,1,1024]{2,0,1:T(8,128)(2,1)S(1)}, bf16[1024,1,1024]{2,0,1:T(8,128)(2,1)}, u32[]{:S(2)}) copy-start(bf16[1024,1,1024]{2,0,1:T(8,128)(2,1)} %convert_bitcast_fusion.1) | copy-start | bytes 6291460
  178.6 404.1 %reduce-scatter.5.cloned.1.call-start = ((), (), s32[]{:S(2)}) async-start(), calls=%async_computation.3 | async-start | bytes 8912896 | tf_op jit(solution)/shard_map/reduce_scatter | solution.py:193
  181.2 3.2 copy-start.31
  183.2 1.2 copy-start.32
  184.3 49.6 %collective-permute-start.4 = (bf16[2,128,1024]{2,1,0:T(8,128)(2,1)}, bf16[2,128,1024]{2,1,0:T(8,128)(2,1)}, u32[]{:S(2)}, u32[]{:S(2)}) collective-permute-start(bf16[2,128,1024]{2,1,0:T(8,128)(2,1)} %get-tuple-element.88), channel_id=1, source_target_pairs={{0,1},{1,2},{2,3},{3,4},{4,5},{5,6},{6,7},{7,8},{8,9},{9,10},{10,1... | collective-permute-start | bytes 1572872 | tf_op jit(solution)/shard_map/ppermute | solution.py:19
  185.3 48.7 %collective-permute-start.5 = (bf16[2,128,1024]{2,1,0:T(8,128)(2,1)}, bf16[2,128,1024]{2,1,0:T(8,128)(2,1)}, u32[]{:S(2)}, u32[]{:S(2)}) collective-permute-start(bf16[2,128,1024]{2,1,0:T(8,128)(2,1)} %get-tuple-element.89), channel_id=1, source_target_pairs={{0,15},{1,0},{2,1},{3,2},{4,3},{5,4},{6,5},{7,6},{8,7},{9,8},{10,9... | collective-permute-start | bytes 1572872 | tf_op jit(solution)/shard_map/ppermute | solution.py:19
  245.6 2.9 copy-start.14
  251.8 4.5 copy-start.19
  256.3 2.5 copy-start.3
  256.3 2.5 copy-start.22
  258.8 1.0 copy-start.24
  258.9 3.2 copy-start.38
  259.8 2.3 copy-start.13
  260.2 3.6 copy-start.25
  260.2 5.7 collective-permute-start.6
  262.1 3.9 copy-start.33
  267.0 2.7 copy-start.16
  282.5 3.7 copy-start.34
  312.1 2.9 copy-start.1
  315.3 5.7 copy-start.2
  316.2 34.3 %collective-permute-start.7 = (bf16[2,128,1024]{2,1,0:T(8,128)(2,1)}, bf16[2,128,1024]{2,1,0:T(8,128)(2,1)}, u32[]{:S(2)}, u32[]{:S(2)}) collective-permute-start(bf16[2,128,1024]{2,1,0:T(8,128)(2,1)} %pad_maximum_fusion.12), channel_id=1, source_target_pairs={{0,15},{1,0},{2,1},{3,2},{4,3},{5,4},{6,5},{7,6},{8,7},{9,8},{10,9... | collective-permute-start | bytes 1572872 | tf_op jit(solution)/shard_map/ppermute | solution.py:19
  320.8 44.0 %collective-permute-start.8 = (bf16[2,128,1024]{2,1,0:T(8,128)(2,1)}, bf16[2,128,1024]{2,1,0:T(8,128)(2,1)}, u32[]{:S(2)}, u32[]{:S(2)}) collective-permute-start(bf16[2,128,1024]{2,1,0:T(8,128)(2,1)} %pad_maximum_fusion.13), channel_id=1, source_target_pairs={{0,1},{1,2},{2,3},{3,4},{4,5},{5,6},{6,7},{7,8},{8,9},{9,10},{10,1... | collective-permute-start | bytes 1572872 | tf_op jit(solution)/shard_map/ppermute | solution.py:19
  341.2 1.0 copy-start.5
  345.8 4.7 copy-start.6
  345.8 4.7 copy-start.10
  366.3 0.8 copy-start.20
  371.0 6.4 %copy-start.12 = (bf16[1024,1,1024]{2,0,1:T(8,128)(2,1)S(1)}, bf16[1024,1,1024]{2,0,1:T(8,128)(2,1)}, u32[]{:S(2)}) copy-start(bf16[1024,1,1024]{2,0,1:T(8,128)(2,1)} %convert_bitcast_fusion) | copy-start | bytes 6291460
  384.1 1.0 copy-start.15
  385.1 2.5 copy-start.8
  385.1 2.5 copy-start.21
  387.7 1.4 copy-start.4
  389.1 1.1 copy-start.17
  390.0 1.1 copy-start.26
Sparse Core Ops, SparseCore 0:
  178.7 221.4 reduce-scatter.2
  402.5 180.1 reduce-scatter.4
where the time goes:
time: 601 us; the launch traced here: 593 us
  waiting for transfers between devices  257 us (43%)
  matrix products  148 us (25%)
  local copies, waits for them, and re-layouts  91.5 us (15%)
  other arithmetic  55.1 us (9%)
  starting transfers between devices  22.2 us (4%)
  between operations  18.8 us (3%)
    reduce_scatter x2, waiting for transfers between devices, per_device(): lax.psum_scatter(tick_rows(jnp.int32(0), features // part_count * lax.axi...  191 us
    ppermute x8, waiting for transfers between devices, from_behind(): return lax.ppermute(value, axis, pairs)  66.5 us
    dot_general x2, matrix products, per_device(): jnp.einsum('bhqk,bqhd->bkhd', scores_bf, query_heads, preferred_element_t...  35.6 us
    dot_general x2, matrix products, per_device(): jnp.einsum('bhqk,bkhd->bqhd', scores_bf, key_heads, preferred_element_typ...  34.4 us
    ppermute x8, starting transfers between devices, from_behind(): return lax.ppermute(value, axis, pairs)  20.3 us
    unnamed x92, local copies, waits for them, and re-layouts  19.5 us
    dot_general x4, matrix products, left_dot(): lax.dot_general(left, right, (((0,), (0,)), ((), ())), preferred_element_...  19.4 us
    dot_general x8, matrix products, right_dot(): lax.dot_general(left, right, (((1,), (1,)), ((), ())), preferred_element_...  15.9 us
  transfers between devices with their start and end apart: 11, of which 6 were waited for; matrix products, arithmetic and copies ran while one was open for 31% of the time, Pallas kernels for 0%

commit v1 on v0

v1 whole, which is shorter than its diff:
```python
import functools
import math

import jax
import jax.numpy as jnp
from jax import lax
from jax.experimental import pallas as pl
from jax.experimental.pallas import tpu as pltpu
from jax.sharding import PartitionSpec as P

HEADS = 8
BLOCK = 128
OFFSETS = (1, -1)
EPSILON = 1e-06
MESH = pl.DeviceIdType.MESH


def from_behind(value, axis, steps):
    count = lax.axis_size(axis)
    pairs = [(source, (source + steps) % count) for source in range(count)]
    return lax.ppermute(value, axis, pairs)


def shifted(x, axis, by):
    size = lax.axis_size(axis)
    pairs = [(i, i + by) for i in range(size) if 0 <= i + by < size]
    return lax.ppermute(x, axis, pairs)


def right_dot(left, right):
    return lax.dot_general(
        left, right, (((1,), (1,)), ((), ())), preferred_element_type=jnp.float32
    )


def left_dot(left, right):
    return lax.dot_general(
        left, right, (((0,), (0,)), ((), ())), preferred_element_type=jnp.float32
    )


def plain_dot(left, right):
    return jnp.dot(left, right, preferred_element_type=jnp.float32)


def attention_kernel(
    scale, q_ref, ko_ref, vo_ref, kh_ref, vh_ref, ga_ref, mask_ref,
    att_ref, gq_ref, kto_ref, vto_ref, kth_ref, vth_ref,
):
    size = BLOCK
    keys = jnp.concatenate([kh_ref[:size], ko_ref[...], kh_ref[size:]], axis=0)
    values = jnp.concatenate([vh_ref[:size], vo_ref[...], vh_ref[size:]], axis=0)
    blocks = q_ref.shape[0] // size
    key_sums = [None] * (blocks + 2)
    value_sums = [None] * (blocks + 2)
    for b in range(blocks):
        rows = slice(b * size, (b + 1) * size)
        near = slice(b * size, (b + 3) * size)
        q = q_ref[rows]
        ga = ga_ref[rows]
        k = keys[near]
        v = values[near]
        scores = right_dot(q, k) * scale + mask_ref[b : b + 1, :]
        raised = jnp.exp(scores - jnp.max(scores, axis=-1, keepdims=True))
        probs = raised / jnp.sum(raised, axis=-1, keepdims=True)
        probs_bf = probs.astype(jnp.bfloat16)
        att_ref[:, rows] = lax.dot_general(
            v, probs_bf, (((0,), (1,)), ((), ())), preferred_element_type=jnp.float32
        ).astype(jnp.bfloat16)
        grad_probs = right_dot(ga, v)
        inner = jnp.sum(probs * grad_probs, axis=-1, keepdims=True)
        scores_bf = (probs * (grad_probs - inner) * scale).astype(jnp.bfloat16)
        gq_ref[rows] = plain_dot(scores_bf, k).astype(jnp.bfloat16)
        key_terms = left_dot(scores_bf, q)
        value_terms = left_dot(probs_bf, ga)
        for j in range(3):
            part = slice(j * size, (j + 1) * size)
            for sums, terms in ((key_sums, key_terms), (value_sums, value_terms)):
                old = sums[b + j]
                sums[b + j] = terms[part] if old is None else old + terms[part]
    for sums, own, halo in ((key_sums, kto_ref, kth_ref), (value_sums, vto_ref, vth_ref)):
        halo[:size] = sums[0].astype(jnp.bfloat16)
        halo[size:] = sums[blocks + 1].astype(jnp.bfloat16)
        for b in range(blocks):
            own[b * size : (b + 1) * size] = sums[b + 1].astype(jnp.bfloat16)


def attention(tick, q, ko, vo, kh, vh, ga, mask):
    rows, features = q.shape[1:]
    dim = features // HEADS
    halo = kh.shape[1]
    ticked = lambda n: pl.BlockSpec((None, n, dim), lambda h: (tick, 0, h))
    flat = lambda n: pl.BlockSpec((n, dim), lambda h: (0, h))
    shape = lambda n: jax.ShapeDtypeStruct((n, features), jnp.bfloat16)
    return pl.pallas_call(
        functools.partial(attention_kernel, 1.0 / math.sqrt(dim)),
        grid=(HEADS,),
        in_specs=[
            ticked(rows), ticked(rows), ticked(rows), ticked(halo), ticked(halo), flat(rows),
            pl.BlockSpec(mask.shape, lambda h: (0, 0)),
        ],
        out_specs=[
            pl.BlockSpec((dim, rows), lambda h: (h, 0)),
            flat(rows), flat(rows), flat(rows), flat(halo), flat(halo),
        ],
        out_shape=[
            jax.ShapeDtypeStruct((features, rows), jnp.bfloat16),
            shape(rows), shape(rows), shape(rows), shape(halo), shape(halo),
        ],
        cost_estimate=pl.CostEstimate(
            flops=12 * rows * 3 * BLOCK * features,
            bytes_accessed=24 * rows * features,
            transcendentals=rows * 3 * BLOCK * HEADS,
        ),
        name="attention_both_ways",
    )(q, ko, vo, kh, vh, ga, mask)


def bit_orders(bits):
    swapped = [1, 0] + list(range(2, bits))
    late = list(range(2, bits)) + [0, 1]
    return (list(range(bits)), swapped, late)


PORTIONS = (
    (0, 0, 0), (0, 1, 1), (3, 1, 2), (1, 0, 0), (1, 1, 1), (2, 0, 0), (2, 1, 1), (3, 0, 0),
)


def weight_kernel(
    count, nown_ref, nhalo_ref, att0_ref, att1_ref, gq0, gq1, up0, up1,
    ko0, ko1, kh0, kh1, vo0, vo1, vh0, vh1,
    out_ref, nlhs, alhs, keep, send, recv, send_sem, recv_sem,
):
    me = lax.axis_index("mesh")
    bits = count.bit_length() - 1
    orders = bit_orders(bits)
    features = nown_ref.shape[0]
    chunk = features // count
    half_columns = features // 2

    def bit_of(b):
        return lax.rem(me // (1 << b), 2)

    def partner(b):
        return me + (1 - 2 * bit_of(b)) * (1 << b)

    barrier = pltpu.get_barrier_semaphore()
    for b in range(bits):
        pl.semaphore_signal(barrier, inc=1, device_id={"mesh": partner(b)}, device_id_type=MESH)
    pl.semaphore_wait(barrier, bits)

    own = nown_ref.shape[1]
    halo = nhalo_ref.shape[1]
    tick = att0_ref.shape[1]

    def chunk_rows(order, place):
        index = 0
        for k, b in enumerate(order):
            here = bit_of(b)
            flip = (place >> (bits - 1 - k)) & 1
            index = index + (1 - here if flip else here) * (1 << b)
        return pl.ds(pl.multiple_of(index * chunk, chunk), chunk)

    def arrange(places):
        for place in places:
            to = slice(place * chunk, (place + 1) * chunk)
            for slot in (0, 1):
                rows = chunk_rows(orders[slot], place)
                nlhs[slot, to, :own] = nown_ref[rows, :]
                nlhs[slot, to, own:] = nhalo_ref[rows, :]
                rows = chunk_rows(orders[2 * slot], place)
                alhs[slot, to, :tick] = att0_ref[rows, :]
                alhs[slot, to, tick:] = att1_ref[rows, :]

    rights = ((gq0, gq1), (ko0, ko1, kh0, kh1), (vo0, vo1, vh0, vh1), (up0, up1))

    def product(portion, rows):
        projection, side, order = portion
        columns = slice(side * half_columns, (side + 1) * half_columns)
        right = jnp.concatenate([r[:, columns] for r in rights[projection]], axis=0)
        if projection == 3:
            left = alhs[0 if order == 0 else 1, rows, :]
        else:
            left = nlhs[order, rows, : right.shape[0]]
        return plain_dot(left, right)

    starts = []
    first = 0
    for k in range(bits):
        starts.append(first)
        first += features >> (k + 1)

    def copy_of(p, k):
        rows = pl.ds(starts[k], features >> (k + 1))
        return pltpu.make_async_remote_copy(
            src_ref=send.at[p, rows],
            dst_ref=recv.at[p, rows],
            send_sem=send_sem.at[p, k],
            recv_sem=recv_sem.at[p, k],
            device_id={"mesh": partner(orders[PORTIONS[p][2]][k])},
            device_id_type=MESH,
        )

    middle = features // 2
    arrange(range(count // 2, count))
    for p, portion in enumerate(PORTIONS):
        send[p, :middle] = product(portion, slice(middle, features)).astype(jnp.bfloat16)
        copy_of(p, 0).start()
    arrange(range(count // 2))
    for p, portion in enumerate(PORTIONS):
        keep[p] = product(portion, slice(0, middle))
    for k in range(bits):
        size = features >> (k + 1)
        for p, (projection, side, _) in enumerate(PORTIONS):
            copy_of(p, k).wait_recv()
            if k + 1 < bits:
                left = size // 2
                send[p, starts[k + 1] : starts[k + 1] + left] = (
                    keep[p, left:size]
                    + recv[p, starts[k] + left : starts[k] + size].astype(jnp.float32)
                ).astype(jnp.bfloat16)
                copy_of(p, k + 1).start()
                keep[p, :left] += recv[p, starts[k] : starts[k] + left].astype(jnp.float32)
            else:
                columns = slice(side * half_columns, (side + 1) * half_columns)
                out_ref[projection, :, columns] = keep[p, :size] + recv[
                    p, starts[k] : starts[k] + size
                ].astype(jnp.float32)
    for k in range(bits):
        for p in range(len(PORTIONS)):
            copy_of(p, k).wait_send()


def weight_sums(normed_own, normed_halo, att, gq, up, ko, kh, vo, vh):
    count = lax.axis_size("mesh")
    bits = count.bit_length() - 1
    features = normed_own.shape[0]
    own = normed_own.shape[1]
    halo = normed_halo.shape[1]
    chunk = features // count
    portions = len(PORTIONS)
    moved = features - chunk
    half_columns = features // 2
    return pl.pallas_call(
        functools.partial(weight_kernel, count),
        out_shape=jax.ShapeDtypeStruct((4, chunk, features), jnp.float32),
        in_specs=[pl.BlockSpec(memory_space=pltpu.VMEM)] * 16,
        out_specs=pl.BlockSpec(memory_space=pltpu.VMEM),
        scratch_shapes=[
            pltpu.VMEM((2, features, own + halo), jnp.bfloat16),
            pltpu.VMEM((2, features, own), jnp.bfloat16),
            pltpu.VMEM((portions, features // 2, half_columns), jnp.float32),
            pltpu.VMEM((portions, moved, half_columns), jnp.bfloat16),
            pltpu.VMEM((portions, moved, half_columns), jnp.bfloat16),
            pltpu.SemaphoreType.DMA((portions, bits)),
            pltpu.SemaphoreType.DMA((portions, bits)),
        ],
        compiler_params=pltpu.CompilerParams(
            collective_id=0, has_side_effects=True, vmem_limit_bytes=56 * 2**20
        ),
        cost_estimate=pl.CostEstimate(
            flops=2 * features * features * (4 * own + 2 * halo),
            bytes_accessed=200 * 2**20,
            transcendentals=0,
        ),
        name="weight_sums",
    )(normed_own, normed_halo, *att, *gq, *up, *ko, *kh, *vo, *vh)


def per_device(
    saved_inputs, w_query, w_key, w_value, w_out, pending, top_grads, key_blocks, counts, plan
):
    sections = lax.axis_size("section")
    section_here = lax.axis_index("section")
    part_here = lax.axis_index("mesh")
    rows_here = pending.shape[1]
    features = pending.shape[2]
    blocks_here = rows_here // BLOCK
    tick_count = plan.shape[0]
    query_weight = w_query[0]
    key_weight = w_key[0]
    value_weight = w_value[0]
    out_weight = w_out[0]
    member_ids = jnp.sum(jnp.where(jnp.arange(sections)[None, :] == section_here, plan, 0), axis=1)
    x_own = jnp.stack(
        [
            lax.dynamic_index_in_dim(saved_inputs[0], member_ids[t], 0, keepdims=False)
            for t in range(tick_count)
        ]
    )
    x_before = from_behind(x_own[:, rows_here - BLOCK :], "mesh", 1)
    x_after = from_behind(x_own[:, :BLOCK], "mesh", -1)

    positions = jnp.arange(BLOCK)
    block_ids = jnp.arange(counts.shape[0])
    global_ids = part_here * blocks_here + jnp.arange(blocks_here)
    own_count = jnp.sum(
        jnp.where(block_ids[None, :] == global_ids[:, None], counts[None, :], 0), axis=1
    )
    listed_counts = jnp.sum(
        jnp.where(block_ids[None, None, :] == key_blocks[:, :, None], counts[None, None, :], 0),
        axis=2,
    )
    near_counts = jnp.stack([listed_counts[:, 1], own_count, listed_counts[:, 0]], axis=1)
    mask = jnp.where(positions[None, None, :] < near_counts[:, :, None], 0.0, -jnp.inf)
    mask = mask.reshape(blocks_here, 3 * BLOCK).astype(jnp.float32)

    def norm(x):
        x_float = x.astype(jnp.float32)
        inv_rms = lax.rsqrt(jnp.mean(x_float * x_float, axis=-1, keepdims=True) + EPSILON)
        normed_float = x_float * inv_rms
        return inv_rms, normed_float, normed_float.astype(jnp.bfloat16)

    def project(normed, weight):
        flat = plain_dot(normed.reshape(-1, features), weight).astype(jnp.bfloat16)
        return flat.reshape(normed.shape)

    inv_rms, normed_float, normed = norm(x_own)
    queries = project(normed, query_weight)
    keys_own = project(normed, key_weight)
    values_own = project(normed, value_weight)
    normed_own_t = normed.reshape(-1, features).T
    x_halo = jnp.concatenate([x_before, x_after], axis=1)
    normed_halo = norm(x_halo)[2]
    keys_halo = project(normed_halo, key_weight)
    values_halo = project(normed_halo, value_weight)
    normed_halo_t = normed_halo.reshape(-1, features).T

    upstream = pending[0]
    outgoing = []
    stored = []
    for t in range(tick_count):
        grad_attended = right_dot(upstream, out_weight).astype(jnp.bfloat16)
        att, gq, ko, vo, kh, vh = attention(
            t, queries, keys_own, values_own, keys_halo, values_halo, grad_attended, mask
        )
        stored.append((att, gq, upstream, ko, kh, vo, vh))
        halo_term = (right_dot(kh, key_weight) + right_dot(vh, value_weight)).astype(jnp.bfloat16)
        from_after = from_behind(halo_term[:BLOCK], "mesh", -1)
        from_before = from_behind(halo_term[BLOCK:], "mesh", 1)
        grad_normed = (
            right_dot(gq, query_weight) + right_dot(ko, key_weight) + right_dot(vo, value_weight)
        )
        middle = jnp.zeros((rows_here - 2 * BLOCK, features), jnp.bfloat16)
        grad_normed = grad_normed + jnp.concatenate(
            [from_before, middle, from_after], axis=0
        ).astype(jnp.float32)
        grad_input = inv_rms[t] * (
            grad_normed
            - normed_float[t]
            * jnp.mean(grad_normed * normed_float[t], axis=-1, keepdims=True)
        )
        grad_x = (upstream.astype(jnp.float32) + grad_input).astype(jnp.bfloat16)
        outgoing.append(grad_x)
        if t + 1 < tick_count:
            passed = shifted(grad_x, "section", -1)
            upstream = jnp.where(section_here == sections - 1, top_grads[t], passed)
    layer_total = weight_sums(normed_own_t, normed_halo_t, *zip(*stored))
    return (layer_total.transpose(1, 0, 2)[None], jnp.stack(outgoing)[:, None])


def solution(mesh):
    in_specs = (
        P("section", None, "mesh", None),
        P("section", None, None),
        P("section", None, None),
        P("section", None, None),
        P("section", None, None),
        P("section", "mesh", None),
        P(None, "mesh", None),
        P("mesh", None),
        P(),
        P(),
    )
    out_specs = (P("section", "mesh", None, None), P(None, "section", "mesh", None))
    return jax.shard_map(
        per_device, mesh=mesh, in_specs=in_specs, out_specs=out_specs, check_vma=False
    )
```

time: 601 us -> 226 us (0.38); the launches traced: 593 us -> 225 us
  waiting for transfers between devices: 257 us -> 19 us
  Pallas kernels: 0 us -> 125 us
  matrix products: 148 us -> 25.4 us
  local copies, waits for them, and re-layouts: 91.5 us -> 12.1 us
  other arithmetic: 55.1 us -> 19.3 us
  between operations: 18.8 us -> 4.87 us
    reduce_scatter x2 -> x0, waiting for transfers between devices: 191 us -> none  [per_device(): lax.psum_scatter(tick_rows(jnp.int32(0), features // part_count * lax.axi...]
    pallas_call x0 -> x3, Pallas kernels: none -> 125 us  [the longest x1 95.6 us: weight_sums(): pl.pallas_call(functools.partial(weight_kernel, count), out_shape=jax.Sha...]
    dot_general x20 -> x5, matrix products: 124 us -> 11.4 us  [plain_dot(): return jnp.dot(left, right, preferred_element_type=jnp.float32)]
    ppermute x8 -> x6, waiting for transfers between devices: 66.5 us -> 19 us  [from_behind(): return lax.ppermute(value, axis, pairs)]
    another operation x18 -> x3, other arithmetic: 23.6 us -> 1.49 us  [the longest x1 1.06 us: per_device(): jnp.stack([lax.dynamic_index_in_dim(saved_inputs[0], member_ids[t], 0, ke...]
    reshape x8 -> x0, local copies, waits for them, and re-layouts: 21.3 us -> none  [the longest x2 9.18 us: per_device(): key_terms = jnp.einsum('bhqk,bqhd->bkhd', scores_bf, query_heads, preferr...]
    concatenate x4 -> x0, other arithmetic: 17 us -> none  [the longest x2 13.5 us: weight_rows(): jnp.concatenate([projected, left_dot(attended, upstream)[:, None]], axis=1)]
    unnamed x92 -> x54, local copies, waits for them, and re-layouts: 19.5 us -> 4.1 us
  transfers between devices with their start and end apart: 11 -> 7, of which waited for: 6 -> 6; matrix products, arithmetic and copies ran while one was open for 31% -> 12% of each run, Pallas kernels for 0% -> 0%
where the time goes in v1:
time: 226 us; the launch traced here: 225 us
  Pallas kernels  125 us (55%)
  matrix products  25.4 us (11%)
  starting transfers between devices  19.6 us (9%)
  other arithmetic  19.3 us (9%)
  waiting for transfers between devices  19 us (8%)
  local copies, waits for them, and re-layouts  12.1 us (5%)
  between operations  4.87 us (2%)
    pallas_call x1, Pallas kernels, weight_sums(): pl.pallas_call(functools.partial(weight_kernel, count), out_shape=jax.Sha...  95.6 us
    pallas_call x2, Pallas kernels, attention(): pl.pallas_call(functools.partial(attention_kernel, 1.0 / math.sqrt(dim)),...  29.1 us
    ppermute x6, waiting for transfers between devices, from_behind(): return lax.ppermute(value, axis, pairs)  19 us
    ppermute x6, starting transfers between devices, from_behind(): return lax.ppermute(value, axis, pairs)  18.3 us
    dot_general x12, matrix products, right_dot(): lax.dot_general(left, right, (((1,), (1,)), ((), ())), preferred_element_...  14 us
    dot_general x5, matrix products, plain_dot(): return jnp.dot(left, right, preferred_element_type=jnp.float32)  11.4 us
    convert_element_type x2, local copies, waits for them, and re-layouts, norm(): x_float = x.astype(jnp.float32)  5.87 us
  transfers between devices with their start and end apart: 7, of which 6 were waited for; matrix products, arithmetic and copies ran while one was open for 12% of the time, Pallas kernels for 0%

profile of v1, /device:TPU:0, one launch (start us, length us, event | category | flops | bytes accessed | tf_op | source)
XLA Modules:
  0.0 224.9 jit_solution(13258501264266090739)
XLA Ops:
  0.6 0.0 copy-start
  0.7 0.9 select_reduce_fusion
  1.6 0.6 fusion.95
  6.1 1.3 dynamic-slice_bitcast_fusion.1
  7.4 1.1 fusion.83
  8.4 2.9 %collective-permute-start = (bf16[2,128,1024]{2,1,0:T(8,128)(2,1)}, bf16[2,128,1024]{2,1,0:T(8,128)(2,1)}, u32[]{:S(2)}, u32[]{:S(2)}) collective-permute-start(bf16[2,128,1024]{2,1,0:T(8,128)(2,1)} %get-tuple-element.36), channel_id=1, source_target_pairs={{0,1},{1,2},{2,3},{3,4},{4,5},{5,6},{6,7},{7,8},{8,9},{9,10},{10,1... | collective-permute-start | bytes 1572872 | tf_op jit(solution)/shard_map/ppermute | solution.py:21
  11.4 4.0 %collective-permute-start.1 = (bf16[2,128,1024]{2,1,0:T(8,128)(2,1)}, bf16[2,128,1024]{2,1,0:T(8,128)(2,1)}, u32[]{:S(2)}, u32[]{:S(2)}) collective-permute-start(bf16[2,128,1024]{2,1,0:T(8,128)(2,1)} %get-tuple-element.37), channel_id=1, source_target_pairs={{0,15},{1,0},{2,1},{3,2},{4,3},{5,4},{6,5},{7,6},{8,7},{9,8},{10,9... | collective-permute-start | bytes 1572872 | tf_op jit(solution)/shard_map/ppermute | solution.py:21
  15.4 0.3 multiply_reduce_fusion.1
  15.6 1.5 fusion.79
  17.1 0.2 fusion.87
  17.3 0.1 copy.24
  17.4 0.2 fusion.86
  17.6 0.1 fusion.94
  17.7 0.1 pad_add_fusion
  17.8 0.1 broadcast_bitcast_fusion
  17.8 2.9 %copy.22 = f32[512,1024]{0,1:T(8,128)} copy(f32[512,1024]{1,0:T(8,128)} %bitcast.152) | data formatting | bytes 4194304 | tf_op jit(solution)/shard_map/convert_element_type | solution.py:310
  20.7 1.6 broadcast_multiply_fusion
  22.3 2.3 %fusion.43 = bf16[512,1024]{1,0:T(8,128)(2,1)} fusion(bf16[512,1024]{1,0:T(8,128)(2,1)S(1)} %bitcast.168, bf16[1,1024,1024]{2,1,0:T(8,128)(2,1)S(1)} %copy-done), kind=kOutput, calls=%fused_computation.42 | convolution fusion | flops 1074266112 | bytes 4194304 | tf_op jit(solution)/shard_map/dot_general | solution.py:43
  24.6 2.3 %fusion.37 = bf16[512,1024]{1,0:T(8,128)(2,1)} fusion(bf16[512,1024]{1,0:T(8,128)(2,1)S(1)} %bitcast.169, bf16[1,1024,1024]{2,1,0:T(8,128)(2,1)S(1)} %copy-done.1), kind=kOutput, calls=%fused_computation.40 | convolution fusion | flops 1074266112 | bytes 4194304 | tf_op jit(solution)/shard_map/dot_general | solution.py:43
  26.9 0.6 compare_select_fusion.mask_ref
  27.5 1.6 fusion.67.ga_ref
  29.2 2.3 %fusion.34 = bf16[512,1024]{1,0:T(8,128)(2,1)} fusion(bf16[512,1024]{1,0:T(8,128)(2,1)S(1)} %bitcast.170, bf16[1,1024,1024]{2,1,0:T(8,128)(2,1)S(1)} %copy-done.6), kind=kOutput, calls=%fused_computation.39 | convolution fusion | flops 1074266112 | bytes 4194304 | tf_op jit(solution)/shard_map/dot_general | solution.py:43
  31.4 2.7 %collective-permute-done = bf16[2,128,1024]{2,1,0:T(8,128)(2,1)} collective-permute-done((bf16[2,128,1024]{2,1,0:T(8,128)(2,1)}, bf16[2,128,1024]{2,1,0:T(8,128)(2,1)}, u32[]{:S(2)}, u32[]{:S(2)}) %collective-permute-start) | collective-permute-done | bytes 524320 | tf_op jit(solution)/shard_map/ppermute | solution.py:21
  34.1 1.9 collective-permute-done.1
  36.0 1.5 multiply_reduce_fusion
  37.5 1.4 multiply_convert_fusion
  39.0 2.3 %fusion.46 = bf16[512,1024]{1,0:T(8,128)(2,1)} fusion(bf16[512,1024]{1,0:T(8,128)(2,1)S(1)} %bitcast.165, bf16[1,1024,1024]{2,1,0:T(8,128)(2,1)S(1)} %copy-done), kind=kOutput, calls=%fused_computation.43 | convolution fusion | flops 1074266112 | bytes 4194304 | tf_op jit(solution)/shard_map/dot_general | solution.py:43
  41.3 2.3 %fusion.40 = bf16[512,1024]{1,0:T(8,128)(2,1)} fusion(bf16[512,1024]{1,0:T(8,128)(2,1)S(1)} %bitcast.166, bf16[1,1024,1024]{2,1,0:T(8,128)(2,1)S(1)} %copy-done.1), kind=kOutput, calls=%fused_computation.41 | convolution fusion | flops 1074266112 | bytes 4194304 | tf_op jit(solution)/shard_map/dot_general | solution.py:43
  43.5 14.5 %attention_both_ways.2 = (bf16[1024,256]{1,0:T(8,128)(2,1)}, bf16[256,1024]{1,0:T(8,128)(2,1)}, bf16[256,1024]{1,0:T(8,128)(2,1)}, bf16[256,1024]{1,0:T(8,128)(2...) custom-call(bf16[2,256,1024]{2,1,0:T(8,128)(2,1)} %bitcast.158, bf16[2,256,1024]{2,1,0:T(8,128)(2,1)} %bitcast.156, ...), custom_call_target="tpu_custom_call" | custom-call | flops 1207959552 | bytes 6291456 | tf_op jit(solution)/shard_map/attention_both_ways/pallas_call | solution.py:95
  58.1 2.6 %fusion.22 = f32[256,1024]{1,0:T(8,128)S(1)} fusion(bf16[256,1024]{1,0:T(8,128)(2,1)} %get-tuple-element.16.ko0, bf16[1,1024,1024]{2,1,0:T(8,128)(2,1)} %param.12), kind=kOutput, calls=%fused_computation.22 | convolution fusion | flops 536870912 | bytes 3670016 | tf_op jit(solution)/shard_map/dot_general | solution.py:31
  60.7 0.0 copy-start.2
  60.7 0.7 fusion.8
  61.4 0.8 copy-done.2
  62.2 0.1 copy-done.18
  62.3 0.7 fusion.76
  63.1 0.0 copy-start.7
  63.2 1.6 collective-permute-start.2
  64.7 4.1 %collective-permute-start.3 = (bf16[128,1024]{1,0:T(8,128)(2,1)S(1)}, bf16[128,1024]{1,0:T(8,128)(2,1)S(1)}, u32[]{:S(2)}, u32[]{:S(2)}) collective-permute-start(bf16[128,1024]{1,0:T(8,128)(2,1)S(1)} %get-tuple-element.41), channel_id=1, source_target_pairs={{0,15},{1,0},{2,1},{3,2},{4,3},{5,4},{6,5},{7,6},{8,7},{9,8},{10,9... | collective-permute-start | bytes 786440 | tf_op jit(solution)/shard_map/ppermute | solution.py:21
  68.8 0.7 fusion.10
  69.6 5.4 %collective-permute-done.2 = bf16[128,1024]{1,0:T(8,128)(2,1)S(1)} collective-permute-done((bf16[128,1024]{1,0:T(8,128)(2,1)S(1)}, bf16[128,1024]{1,0:T(8,128)(2,1)S(1)}, u32[]{:S(2)}, u32[]{:S(2)}) %collective-permute-start.2) | collective-permute-done | bytes 262176 | tf_op jit(solution)/shard_map/ppermute | solution.py:21
  75.0 1.9 collective-permute-done.3
  76.9 1.0 multiply_reduce_fusion.3
  77.9 0.3 add_convert_fusion.1
  78.2 1.3 collective-permute-start.4
  79.5 2.8 %maximum_convert_fusion = f32[2,256,1024]{2,1,0:T(8,128)} fusion(bf16[2,128,1024]{2,1,0:T(8,128)(2,1)} %collective-permute-done.1, bf16[2,128,1024]{2,1,0:T(8,128)(2,1)} %collective-permute-done), kind=kLoop, calls=%fused_computation.64 | loop fusion | flops 2097152 | bytes 3145728 | tf_op jit(solution)/shard_map/convert_element_type | solution.py:310
  82.4 3.0 %copy.23 = f32[512,1024]{0,1:T(8,128)} copy(f32[512,1024]{1,0:T(8,128)} %bitcast.153) | data formatting | bytes 4194304 | tf_op jit(solution)/shard_map/convert_element_type | solution.py:310
  85.4 4.3 %fusion.80 = (bf16[1024,512]{1,0:T(8,128)(2,1)}, bf16[1024,512]{1,0:T(8,128)(2,1)}) fusion(f32[512,1024]{0,1:T(8,128)} %copy.22, f32[512]{0:T(512)S(1)} %bitcast.172, f32[512,1024]{0,1:T(8,128)} %copy.23, f32[512]{0:T(512)S(1)} %bitcast.173), kind=kLoop, calls=%fused_computation.60 | loop fusion | flops 2097152 | bytes 6295552 | tf_op jit(solution)/shard_map/transpose | solution.py:323
  89.6 1.1 bitcast_select_fusion.up1
  90.7 1.6 fusion.70.ga_ref
  92.3 14.6 %attention_both_ways.3 = (bf16[1024,256]{1,0:T(8,128)(2,1)}, bf16[256,1024]{1,0:T(8,128)(2,1)}, bf16[256,1024]{1,0:T(8,128)(2,1)}, bf16[256,1024]{1,0:T(8,128)(2...) custom-call(bf16[2,256,1024]{2,1,0:T(8,128)(2,1)} %bitcast.159, bf16[2,256,1024]{2,1,0:T(8,128)(2,1)} %bitcast.157, ...), custom_call_target="tpu_custom_call" | custom-call | flops 1207959552 | bytes 6291456 | tf_op jit(solution)/shard_map/attention_both_ways/pallas_call | solution.py:95
  106.9 1.8 fusion.4
  108.7 0.7 fusion.6
  109.5 95.6 %weight_sums.1 = f32[4,64,1024]{2,1,0:T(8,128)} custom-call(bf16[1024,512]{1,0:T(8,128)(2,1)} %get-tuple-element.56.nown_ref, bf16[1024,512]{1,0:T(8,128)(2,1)} %get-tuple-element.57.nhalo_ref, bf16[1024,256]{1,0:T(8,128)(2,1)} %get-tuple-element.14.att0_ref, bf16[1024,256]{1,0:T(8,128)(2,1)} %get-tuple-element.20.att1_ref, ...), custom_call_target="tpu_custom_call" | custom-call | flops 6442450944 | bytes 209715200 | tf_op jit(solution)/shard_map/weight_sums/pallas_call | solution.py:245
  205.1 0.0 copy-start.3
  205.1 3.0 %copy.25 = f32[1,64,4,1024]{3,2,1,0:T(4,128)} copy(f32[1,64,4,1024]{3,1,2,0:T(8,128)} %bitcast.167) | data formatting | bytes 2097152
  208.2 0.8 fusion.73
  209.0 1.6 collective-permute-start.5
  210.6 4.0 %collective-permute-start.6 = (bf16[128,1024]{1,0:T(8,128)(2,1)S(1)}, bf16[128,1024]{1,0:T(8,128)(2,1)S(1)}, u32[]{:S(2)}, u32[]{:S(2)}) collective-permute-start(bf16[128,1024]{1,0:T(8,128)(2,1)S(1)} %get-tuple-element.39), channel_id=1, source_target_pairs={{0,15},{1,0},{2,1},{3,2},{4,3},{5,4},{6,5},{7,6},{8,7},{9,8},{10,9... | collective-permute-start | bytes 786440 | tf_op jit(solution)/shard_map/ppermute | solution.py:21
  214.7 0.7 fusion.18
  215.4 6.2 %collective-permute-done.5 = bf16[128,1024]{1,0:T(8,128)(2,1)S(1)} collective-permute-done((bf16[128,1024]{1,0:T(8,128)(2,1)S(1)}, bf16[128,1024]{1,0:T(8,128)(2,1)S(1)}, u32[]{:S(2)}, u32[]{:S(2)}) %collective-permute-start.5) | collective-permute-done | bytes 262176 | tf_op jit(solution)/shard_map/ppermute | solution.py:21
  221.7 0.8 collective-permute-done.6
  222.5 1.0 multiply_reduce_fusion.2
  223.5 0.4 fusion.82
  223.9 1.1 maximum_bitcast_fusion
  (57 shorter events, 0.2 us)
Async XLA Ops:
  0.6 21.7 %copy-start = (bf16[1,1024,1024]{2,1,0:T(8,128)(2,1)S(1)}, bf16[1,1024,1024]{2,1,0:T(8,128)(2,1)}, u32[]{:S(2)}) copy-start(bf16[1,1024,1024]{2,1,0:T(8,128)(2,1)} %param.13) | copy-start | bytes 6291460
  8.4 25.7 %collective-permute-start = (bf16[2,128,1024]{2,1,0:T(8,128)(2,1)}, bf16[2,128,1024]{2,1,0:T(8,128)(2,1)}, u32[]{:S(2)}, u32[]{:S(2)}) collective-permute-start(bf16[2,128,1024]{2,1,0:T(8,128)(2,1)} %get-tuple-element.36), channel_id=1, source_target_pairs={{0,1},{1,2},{2,3},{3,4},{4,5},{5,6},{6,7},{7,8},{8,9},{9,10},{10,1... | collective-permute-start | bytes 1572872 | tf_op jit(solution)/shard_map/ppermute | solution.py:21
  11.4 24.7 %collective-permute-start.1 = (bf16[2,128,1024]{2,1,0:T(8,128)(2,1)}, bf16[2,128,1024]{2,1,0:T(8,128)(2,1)}, u32[]{:S(2)}, u32[]{:S(2)}) collective-permute-start(bf16[2,128,1024]{2,1,0:T(8,128)(2,1)} %get-tuple-element.37), channel_id=1, source_target_pairs={{0,15},{1,0},{2,1},{3,2},{4,3},{5,4},{6,5},{7,6},{8,7},{9,8},{10,9... | collective-permute-start | bytes 1572872 | tf_op jit(solution)/shard_map/ppermute | solution.py:21
  15.4 1.8 copy-start.22
  15.4 2.0 copy-start.21
  22.3 2.3 %copy-start.1 = (bf16[1,1024,1024]{2,1,0:T(8,128)(2,1)S(1)}, bf16[1,1024,1024]{2,1,0:T(8,128)(2,1)}, u32[]{:S(2)}) copy-start(bf16[1,1024,1024]{2,1,0:T(8,128)(2,1)} %param.12) | copy-start | bytes 6291460
  24.6 2.9 %copy-start.11 = (bf16[1,256,1024]{2,1,0:T(8,128)(2,1)S(1)}, bf16[1,256,1024]{2,1,0:T(8,128)(2,1)}, u32[]{:S(2)}) copy-start(bf16[1,256,1024]{2,1,0:T(8,128)(2,1)} %param.15) | copy-start | bytes 1572868
  24.6 2.9 %copy-start.23 = (bf16[1,1024,1024]{2,1,0:T(8,128)(2,1)S(1)}, bf16[1,1024,1024]{2,1,0:T(8,128)(2,1)}, u32[]{:S(2)}) copy-start(bf16[1,1024,1024]{2,1,0:T(8,128)(2,1)} %param.14) | copy-start | bytes 6291460
  26.9 2.2 copy-start.6
  58.1 2.6 %copy-start.13 = (bf16[256,1024]{1,0:T(8,128)(2,1)S(1)}, bf16[256,1024]{1,0:T(8,128)(2,1)}, u32[]{:S(2)}) copy-start(bf16[256,1024]{1,0:T(8,128)(2,1)} %get-tuple-element.19.vh0) | copy-start | bytes 1572868
  60.7 1.6 copy-start.2
  60.7 1.7 copy-start.18
  62.3 6.5 %copy-start.12 = (bf16[256,1024]{1,0:T(8,128)(2,1)S(1)}, bf16[256,1024]{1,0:T(8,128)(2,1)}, u32[]{:S(2)}) copy-start(bf16[256,1024]{1,0:T(8,128)(2,1)} %get-tuple-element.17.vo0) | copy-start | bytes 1572868
  63.1 13.8 %copy-start.7 = (bf16[1,1024,1024]{2,1,0:T(8,128)(2,1)S(1)}, bf16[1,1024,1024]{2,1,0:T(8,128)(2,1)}, u32[]{:S(2)}) copy-start(bf16[1,1024,1024]{2,1,0:T(8,128)(2,1)} %param.11) | copy-start | bytes 6291460
  63.1 13.8 %copy-start.4 = (f32[2,256,1024]{2,1,0:T(8,128)S(1)}, f32[2,256,1024]{2,1,0:T(8,128)}, u32[]{:S(2)}) copy-start(f32[2,256,1024]{2,1,0:T(8,128)} %get-tuple-element.34) | copy-start | bytes 6291460
  63.1 13.8 %copy-start.17 = (bf16[256,1024]{1,0:T(8,128)(2,1)S(1)}, bf16[256,1024]{1,0:T(8,128)(2,1)}, u32[]{:S(2)}) copy-start(bf16[256,1024]{1,0:T(8,128)(2,1)} %get-tuple-element.15.gq0) | copy-start | bytes 1572868
  63.2 11.9 %collective-permute-start.2 = (bf16[128,1024]{1,0:T(8,128)(2,1)S(1)}, bf16[128,1024]{1,0:T(8,128)(2,1)S(1)}, u32[]{:S(2)}, u32[]{:S(2)}) collective-permute-start(bf16[128,1024]{1,0:T(8,128)(2,1)S(1)} %get-tuple-element.40), channel_id=1, source_target_pairs={{0,1},{1,2},{2,3},{3,4},{4,5},{5,6},{6,7},{7,8},{8,9},{9,10},{10,1... | collective-permute-start | bytes 786440 | tf_op jit(solution)/shard_map/ppermute | solution.py:21
  64.7 12.2 %collective-permute-start.3 = (bf16[128,1024]{1,0:T(8,128)(2,1)S(1)}, bf16[128,1024]{1,0:T(8,128)(2,1)S(1)}, u32[]{:S(2)}, u32[]{:S(2)}) collective-permute-start(bf16[128,1024]{1,0:T(8,128)(2,1)S(1)} %get-tuple-element.41), channel_id=1, source_target_pairs={{0,15},{1,0},{2,1},{3,2},{4,3},{5,4},{6,5},{7,6},{8,7},{9,8},{10,9... | collective-permute-start | bytes 786440 | tf_op jit(solution)/shard_map/ppermute | solution.py:21
  78.2 11.4 %collective-permute-start.4 = (bf16[256,1024]{1,0:T(8,128)(2,1)S(1)}, bf16[256,1024]{1,0:T(8,128)(2,1)}, u32[]{:S(2)}, u32[]{:S(2)}) collective-permute-start(bf16[256,1024]{1,0:T(8,128)(2,1)S(1)} %add_convert_fusion.1), channel_id=1, source_target_pairs={{16,0},{17,1},{18,2},{19,3},{20,4},{21,5},{22,6},{23,7},{24,8},{25... | collective-permute-start | bytes 1572872 | tf_op jit(solution)/shard_map/ppermute | solution.py:27
  85.3 4.3 %copy-start.16 = (bf16[1,256,1024]{2,1,0:T(8,128)(2,1)S(1)}, bf16[1,256,1024]{2,1,0:T(8,128)(2,1)}, u32[]{:S(2)}) copy-start(bf16[1,256,1024]{2,1,0:T(8,128)(2,1)} %param.16) | copy-start | bytes 1572868
  85.4 5.4 %copy-start.24 = (bf16[1,1024,1024]{2,1,0:T(8,128)(2,1)S(1)}, bf16[1,1024,1024]{2,1,0:T(8,128)(2,1)}, u32[]{:S(2)}) copy-start(bf16[1,1024,1024]{2,1,0:T(8,128)(2,1)} %param.14) | copy-start | bytes 6291460
  90.7 16.1 %copy-start.9 = (bf16[256,1024]{1,0:T(8,128)(2,1)}, bf16[256,1024]{1,0:T(8,128)(2,1)S(1)}, u32[]{:S(2)}) copy-start(bf16[256,1024]{1,0:T(8,128)(2,1)S(1)} %bitcast_select_fusion.up1) | copy-start | bytes 1572868
  106.9 1.9 copy-start.15
  109.5 98.7 %copy-start.20 = (bf16[256,1024]{1,0:T(8,128)(2,1)S(1)}, bf16[256,1024]{1,0:T(8,128)(2,1)}, u32[]{:S(2)}) copy-start(bf16[256,1024]{1,0:T(8,128)(2,1)} %get-tuple-element.23.kh1) | copy-start | bytes 1572868
  205.1 3.0 %copy-start.3 = (bf16[1,1024,1024]{2,1,0:T(8,128)(2,1)S(1)}, bf16[1,1024,1024]{2,1,0:T(8,128)(2,1)}, u32[]{:S(2)}) copy-start(bf16[1,1024,1024]{2,1,0:T(8,128)(2,1)} %param.12) | copy-start | bytes 6291460
  208.2 6.5 %copy-start.14 = (bf16[256,1024]{1,0:T(8,128)(2,1)S(1)}, bf16[256,1024]{1,0:T(8,128)(2,1)}, u32[]{:S(2)}) copy-start(bf16[256,1024]{1,0:T(8,128)(2,1)} %get-tuple-element.22.ko1) | copy-start | bytes 1572868
  208.9 13.6 %copy-start.8 = (bf16[1,1024,1024]{2,1,0:T(8,128)(2,1)S(1)}, bf16[1,1024,1024]{2,1,0:T(8,128)(2,1)}, u32[]{:S(2)}) copy-start(bf16[1,1024,1024]{2,1,0:T(8,128)(2,1)} %param.11) | copy-start | bytes 6291460
  209.0 13.5 %copy-start.5 = (f32[2,256,1024]{2,1,0:T(8,128)S(1)}, f32[2,256,1024]{2,1,0:T(8,128)}, u32[]{:S(2)}) copy-start(f32[2,256,1024]{2,1,0:T(8,128)} %get-tuple-element.34) | copy-start | bytes 6291460
  209.0 13.5 %copy-start.19 = (bf16[256,1024]{1,0:T(8,128)(2,1)S(1)}, bf16[256,1024]{1,0:T(8,128)(2,1)}, u32[]{:S(2)}) copy-start(bf16[256,1024]{1,0:T(8,128)(2,1)} %get-tuple-element.21.gq1) | copy-start | bytes 1572868
  209.0 12.7 %collective-permute-start.5 = (bf16[128,1024]{1,0:T(8,128)(2,1)S(1)}, bf16[128,1024]{1,0:T(8,128)(2,1)S(1)}, u32[]{:S(2)}, u32[]{:S(2)}) collective-permute-start(bf16[128,1024]{1,0:T(8,128)(2,1)S(1)} %get-tuple-element.38), channel_id=1, source_target_pairs={{0,1},{1,2},{2,3},{3,4},{4,5},{5,6},{6,7},{7,8},{8,9},{9,10},{10,1... | collective-permute-start | bytes 786440 | tf_op jit(solution)/shard_map/ppermute | solution.py:21
  210.6 11.9 %collective-permute-start.6 = (bf16[128,1024]{1,0:T(8,128)(2,1)S(1)}, bf16[128,1024]{1,0:T(8,128)(2,1)S(1)}, u32[]{:S(2)}, u32[]{:S(2)}) collective-permute-start(bf16[128,1024]{1,0:T(8,128)(2,1)S(1)} %get-tuple-element.39), channel_id=1, source_target_pairs={{0,15},{1,0},{2,1},{3,2},{4,3},{5,4},{6,5},{7,6},{8,7},{9,8},{10,9... | collective-permute-start | bytes 786440 | tf_op jit(solution)/shard_map/ppermute | solution.py:21
  215.4 8.1 %copy-start.10 = (bf16[256,1024]{1,0:T(8,128)(2,1)S(1)}, bf16[256,1024]{1,0:T(8,128)(2,1)}, u32[]{:S(2)}) copy-start(bf16[256,1024]{1,0:T(8,128)(2,1)} %copy-done.9) | copy-start | bytes 1572868

commit v2 on v1

v2 whole, which is shorter than its diff:
```python
import functools
import math

import jax
import jax.numpy as jnp
from jax import lax
from jax.experimental import pallas as pl
from jax.experimental.pallas import tpu as pltpu
from jax.sharding import PartitionSpec as P

HEADS = 8
BLOCK = 128
OFFSETS = (1, -1)
EPSILON = 1e-06
MESH = pl.DeviceIdType.MESH


def from_behind(value, axis, steps):
    count = lax.axis_size(axis)
    pairs = [(source, (source + steps) % count) for source in range(count)]
    return lax.ppermute(value, axis, pairs)


def shifted(x, axis, by):
    size = lax.axis_size(axis)
    pairs = [(i, i + by) for i in range(size) if 0 <= i + by < size]
    return lax.ppermute(x, axis, pairs)


def right_dot(left, right):
    return lax.dot_general(
        left, right, (((1,), (1,)), ((), ())), preferred_element_type=jnp.float32
    )


def left_dot(left, right):
    return lax.dot_general(
        left, right, (((0,), (0,)), ((), ())), preferred_element_type=jnp.float32
    )


def plain_dot(left, right):
    return jnp.dot(left, right, preferred_element_type=jnp.float32)


def near_keys(own_ref, halo_ref, columns):
    return jnp.concatenate(
        [halo_ref[:BLOCK, columns], own_ref[:, columns], halo_ref[BLOCK:, columns]], axis=0
    )


def softmax(q, k, mask, scale):
    scores = right_dot(q, k) * scale + mask
    raised = jnp.exp(scores - jnp.max(scores, axis=-1, keepdims=True))
    return raised / jnp.sum(raised, axis=-1, keepdims=True)


def head_forward(scale, q_ref, ko_ref, vo_ref, kh_ref, vh_ref, mask_ref, att_ref):
    every = slice(None)
    keys = near_keys(ko_ref, kh_ref, every)
    values = near_keys(vo_ref, vh_ref, every)
    for b in range(q_ref.shape[0] // BLOCK):
        rows = slice(b * BLOCK, (b + 1) * BLOCK)
        near = slice(b * BLOCK, (b + 3) * BLOCK)
        probs = softmax(q_ref[rows], keys[near], mask_ref[b : b + 1, :], scale)
        att_ref[:, rows] = lax.dot_general(
            values[near], probs.astype(jnp.bfloat16), (((0,), (1,)), ((), ())),
            preferred_element_type=jnp.float32,
        ).astype(jnp.bfloat16)


def head_backward(
    scale, columns, q_ref, ko_ref, vo_ref, kh_ref, vh_ref, ga_ref, mask_ref,
    gq_ref, kto_ref, vto_ref, kth_ref, vth_ref, att_ref=None,
):
    size = BLOCK
    keys = near_keys(ko_ref, kh_ref, columns)
    values = near_keys(vo_ref, vh_ref, columns)
    blocks = q_ref.shape[0] // size
    key_sums = [None] * (blocks + 2)
    value_sums = [None] * (blocks + 2)
    for b in range(blocks):
        rows = slice(b * size, (b + 1) * size)
        near = slice(b * size, (b + 3) * size)
        q = q_ref[rows, columns]
        ga = ga_ref[rows, columns]
        k = keys[near]
        v = values[near]
        probs = softmax(q, k, mask_ref[b : b + 1, :], scale)
        probs_bf = probs.astype(jnp.bfloat16)
        if att_ref is not None:
            att_ref[:, rows] = lax.dot_general(
                v, probs_bf, (((0,), (1,)), ((), ())), preferred_element_type=jnp.float32
            ).astype(jnp.bfloat16)
        grad_probs = right_dot(ga, v)
        inner = jnp.sum(probs * grad_probs, axis=-1, keepdims=True)
        scores_bf = (probs * (grad_probs - inner) * scale).astype(jnp.bfloat16)
        gq_ref[rows, columns] = plain_dot(scores_bf, k).astype(jnp.bfloat16)
        key_terms = left_dot(scores_bf, q)
        value_terms = left_dot(probs_bf, ga)
        for j in range(3):
            part = slice(j * size, (j + 1) * size)
            for sums, terms in ((key_sums, key_terms), (value_sums, value_terms)):
                old = sums[b + j]
                sums[b + j] = terms[part] if old is None else old + terms[part]
    for sums, own, halo in ((key_sums, kto_ref, kth_ref), (value_sums, vto_ref, vth_ref)):
        halo[:size, columns] = sums[0].astype(jnp.bfloat16)
        halo[size:, columns] = sums[blocks + 1].astype(jnp.bfloat16)
        for b in range(blocks):
            own[b * size : (b + 1) * size, columns] = sums[b + 1].astype(jnp.bfloat16)


def turn(from_ref, to_ref):
    rows = from_ref.shape[0]
    down = lax.broadcasted_iota(jnp.int32, (rows, rows), 0)
    across = lax.broadcasted_iota(jnp.int32, (rows, rows), 1)
    identity = jnp.where(down == across, 1.0, 0.0).astype(jnp.bfloat16)
    to_ref[...] = left_dot(from_ref[...], identity).astype(jnp.bfloat16)


def forward_kernel(scale, q, ko, vo, kh, vh, mask, no, nh, att, not_, nht):
    head_forward(scale, q, ko, vo, kh, vh, mask, att)
    turn(no, not_)
    turn(nh, nht)


def both_kernel(
    scale, q, ko, vo, kh, vh, mask, no, nh, ga, att, not_, nht, gq, kto, vto, kth, vth
):
    head_backward(
        scale, slice(None), q, ko, vo, kh, vh, ga, mask, gq, kto, vto, kth, vth, att
    )
    turn(no, not_)
    turn(nh, nht)


def attention(q, ko, vo, kh, vh, mask, no, nh, ga=None):
    rows, features = q.shape
    dim = features // HEADS
    halo = kh.shape[0]
    flat = lambda n: pl.BlockSpec((n, dim), lambda h: (0, h))
    tall = lambda n: pl.BlockSpec((dim, n), lambda h: (h, 0))
    shape = lambda n: jax.ShapeDtypeStruct((n, features), jnp.bfloat16)
    tall_shape = lambda n: jax.ShapeDtypeStruct((features, n), jnp.bfloat16)
    in_specs = [flat(rows), flat(rows), flat(rows), flat(halo), flat(halo)]
    in_specs += [pl.BlockSpec(mask.shape, lambda h: (0, 0)), flat(rows), flat(halo)]
    out_specs = [tall(rows), tall(rows), tall(halo)]
    out_shape = [tall_shape(rows), tall_shape(rows), tall_shape(halo)]
    operands = [q, ko, vo, kh, vh, mask, no, nh]
    if ga is not None:
        in_specs.append(flat(rows))
        operands.append(ga)
        out_specs += [flat(rows), flat(rows), flat(rows), flat(halo), flat(halo)]
        out_shape += [shape(rows), shape(rows), shape(rows), shape(halo), shape(halo)]
    return pl.pallas_call(
        functools.partial(
            forward_kernel if ga is None else both_kernel, 1.0 / math.sqrt(dim)
        ),
        grid=(HEADS,),
        in_specs=in_specs,
        out_specs=out_specs,
        out_shape=out_shape,
        cost_estimate=pl.CostEstimate(
            flops=(4 if ga is None else 12) * rows * 3 * BLOCK * features,
            bytes_accessed=24 * rows * features,
            transcendentals=rows * 3 * BLOCK * HEADS,
        ),
        name="attention_forward" if ga is None else "attention_both_ways",
    )(*operands)


def bit_orders(bits):
    swapped = [1, 0] + list(range(2, bits))
    late = list(range(2, bits)) + [0, 1]
    return (list(range(bits)), swapped, late)


QUARTERS = 4
PORTIONS = ((3, 0, 0), (3, 1, 1), (3, 2, 2), (3, 3, 2)) + tuple(
    (projection, quarter, quarter % 2) for projection in range(3) for quarter in range(QUARTERS)
)
EARLY = 4


def last_kernel(
    count, n0, nh0, n1, nh1, att0, att1, gq0, ko0, vo0, kh0, vh0, up0, up1,
    q1, key1, value1, key_halo1, value_halo1, mask, x1, wq, wk, wv, wo,
    out_ref, grad_x_ref,
    nlhs, alhs, keep, send, recv, ga1, gq1, ko1, vo1, kh1, vh1, term, term_in,
    send_sem, recv_sem, term_send, term_recv,
):
    me = lax.axis_index("mesh")
    bits = count.bit_length() - 1
    orders = bit_orders(bits)
    features = n0.shape[0]
    rows_here = x1.shape[0]
    chunk = features // count
    width = features // QUARTERS
    scale = 1.0 / math.sqrt(features // HEADS)
    after = lax.rem(me + 1, count)
    before = lax.rem(me + count - 1, count)

    def bit_of(b):
        return lax.rem(me // (1 << b), 2)

    def partner(b):
        return me + (1 - 2 * bit_of(b)) * (1 << b)

    barrier = pltpu.get_barrier_semaphore()
    for other in [before, after] + [partner(b) for b in range(bits)]:
        pl.semaphore_signal(barrier, inc=1, device_id={"mesh": other}, device_id_type=MESH)

    def chunk_rows(order, place):
        index = 0
        for k, b in enumerate(order):
            here = bit_of(b)
            flip = (place >> (bits - 1 - k)) & 1
            index = index + (1 - here if flip else here) * (1 << b)
        return pl.ds(pl.multiple_of(index * chunk, chunk), chunk)

    def arrange(to_ref, slot, order, parts):
        for place in range(count):
            rows = chunk_rows(order, place)
            first = 0
            for part in parts:
                last = first + part.shape[1]
                to_ref[slot, place * chunk : (place + 1) * chunk, first:last] = part[rows, :]
                first = last

    rights = ((gq0, gq1), (ko0, ko1, kh0, kh1), (vo0, vo1, vh0, vh1), (up0, up1))

    def columns_of(portion):
        return slice(portion[1] * width, (portion[1] + 1) * width)

    def product(portion, rows):
        projection, _, order = portion
        right = jnp.concatenate([r[:, columns_of(portion)] for r in rights[projection]], axis=0)
        left = alhs if projection == 3 else nlhs
        return plain_dot(left[order, rows, : right.shape[0]], right)

    starts = []
    first = 0
    for k in range(bits):
        starts.append(first)
        first += features >> (k + 1)

    def copy_of(p, k):
        rows = pl.ds(starts[k], features >> (k + 1))
        return pltpu.make_async_remote_copy(
            src_ref=send.at[p, rows],
            dst_ref=recv.at[p, rows],
            send_sem=send_sem.at[p, k],
            recv_sem=recv_sem.at[p, k],
            device_id={"mesh": partner(orders[PORTIONS[p][2]][k])},
            device_id_type=MESH,
        )

    def term_copy(side):
        return pltpu.make_async_remote_copy(
            src_ref=term.at[pl.ds(side * BLOCK, BLOCK)],
            dst_ref=term_in.at[pl.ds((1 - side) * BLOCK, BLOCK)],
            send_sem=term_send.at[side],
            recv_sem=term_recv.at[1 - side],
            device_id={"mesh": after if side else before},
            device_id_type=MESH,
        )

    def arrived(side):
        return term_copy(1 - side)

    middle = features // 2

    def begin(p):
        send[p, :middle] = product(PORTIONS[p], slice(middle, features)).astype(jnp.bfloat16)
        copy_of(p, 0).start()

    for slot, order in enumerate(orders):
        arrange(alhs, slot, order, (att0, att1))
    pl.semaphore_wait(barrier, bits + 2)
    for p in range(EARLY):
        begin(p)

    ga1[...] = right_dot(up1[...], wo[...]).astype(jnp.bfloat16)
    dim = features // HEADS

    @pl.loop(0, HEADS)
    def _(h):
        columns = pl.ds(pl.multiple_of(h * dim, dim), dim)
        head_backward(
            scale, columns, q1, key1, value1, key_halo1, value_halo1, ga1, mask,
            gq1, ko1, vo1, kh1, vh1,
        )

    term[...] = (right_dot(kh1[...], wk[...]) + right_dot(vh1[...], wv[...])).astype(jnp.bfloat16)
    for side in (0, 1):
        term_copy(side).start()
    for slot in (0, 1):
        arrange(nlhs, slot, orders[slot], (n0, n1, nh0, nh1))
    for p in range(EARLY, len(PORTIONS)):
        begin(p)
    for p, portion in enumerate(PORTIONS):
        keep[p] = product(portion, slice(0, middle))

    def finish_input():
        x_float = x1[...].astype(jnp.float32)
        inv_rms = lax.rsqrt(jnp.mean(x_float * x_float, axis=-1, keepdims=True) + EPSILON)
        normed = x_float * inv_rms
        grad = right_dot(gq1[...], wq[...])
        grad = grad + right_dot(ko1[...], wk[...]) + right_dot(vo1[...], wv[...])
        for side in (0, 1):
            arrived(side).wait_recv()
        pieces = [term_in[:BLOCK].astype(jnp.float32)]
        if rows_here > 2 * BLOCK:
            pieces.append(jnp.zeros((rows_here - 2 * BLOCK, features), jnp.float32))
        pieces.append(term_in[BLOCK:].astype(jnp.float32))
        grad = grad + jnp.concatenate(pieces, axis=0)
        grad = inv_rms * (grad - normed * jnp.mean(grad * normed, axis=-1, keepdims=True))
        grad_x_ref[...] = (up1[...].astype(jnp.float32) + grad).astype(jnp.bfloat16)

    for k in range(bits):
        size = features >> (k + 1)
        for p, portion in enumerate(PORTIONS):
            copy_of(p, k).wait_recv()
            if k + 1 < bits:
                left = size // 2
                send[p, starts[k + 1] : starts[k + 1] + left] = (
                    keep[p, left:size]
                    + recv[p, starts[k] + left : starts[k] + size].astype(jnp.float32)
                ).astype(jnp.bfloat16)
                copy_of(p, k + 1).start()
                keep[p, :left] += recv[p, starts[k] : starts[k] + left].astype(jnp.float32)
            else:
                out_ref[:, portion[0], columns_of(portion)] = keep[p, :size] + recv[
                    p, starts[k] : starts[k] + size
                ].astype(jnp.float32)
        if k == 0:
            finish_input()
    for k in range(bits):
        for p in range(len(PORTIONS)):
            copy_of(p, k).wait_send()
    for side in (0, 1):
        term_copy(side).wait_send()


def last_tick(*operands):
    count = lax.axis_size("mesh")
    bits = count.bit_length() - 1
    features, rows = operands[0].shape
    halo = operands[1].shape[1]
    chunk = features // count
    portions = len(PORTIONS)
    moved = features - chunk
    width = features // QUARTERS
    half = lambda *shape: pltpu.VMEM(shape, jnp.bfloat16)
    return pl.pallas_call(
        functools.partial(last_kernel, count),
        out_shape=[
            jax.ShapeDtypeStruct((chunk, 4, features), jnp.float32),
            jax.ShapeDtypeStruct((rows, features), jnp.bfloat16),
        ],
        in_specs=[pl.BlockSpec(memory_space=pltpu.VMEM)] * len(operands),
        out_specs=[pl.BlockSpec(memory_space=pltpu.VMEM)] * 2,
        scratch_shapes=[
            half(2, features, 2 * (rows + halo)),
            half(3, features, 2 * rows),
            pltpu.VMEM((portions, features // 2, width), jnp.float32),
            half(portions, moved, width),
            half(portions, moved, width),
            half(rows, features),
            half(rows, features),
            half(rows, features),
            half(rows, features),
            half(halo, features),
            half(halo, features),
            half(halo, features),
            half(halo, features),
            pltpu.SemaphoreType.DMA((portions, bits)),
            pltpu.SemaphoreType.DMA((portions, bits)),
            pltpu.SemaphoreType.DMA((2,)),
            pltpu.SemaphoreType.DMA((2,)),
        ],
        compiler_params=pltpu.CompilerParams(
            collective_id=0, has_side_effects=True, vmem_limit_bytes=60 * 2**20
        ),
        cost_estimate=pl.CostEstimate(
            flops=4 * features * features * (4 * rows + 2 * halo),
            bytes_accessed=200 * 2**20,
            transcendentals=0,
        ),
        name="last_tick",
    )(*operands)


def per_device(
    saved_inputs, w_query, w_key, w_value, w_out, pending, top_grads, key_blocks, counts, plan
):
    sections = lax.axis_size("section")
    section_here = lax.axis_index("section")
    part_here = lax.axis_index("mesh")
    rows_here = pending.shape[1]
    features = pending.shape[2]
    blocks_here = rows_here // BLOCK
    query_weight = w_query[0]
    key_weight = w_key[0]
    value_weight = w_value[0]
    out_weight = w_out[0]

    def norm(x):
        x_float = x.astype(jnp.float32)
        inv_rms = lax.rsqrt(jnp.mean(x_float * x_float, axis=-1, keepdims=True) + EPSILON)
        normed_float = x_float * inv_rms
        return inv_rms, normed_float, normed_float.astype(jnp.bfloat16)

    def project(normed, weight):
        return plain_dot(normed, weight).astype(jnp.bfloat16)

    members = lax.dynamic_index_in_dim(plan, section_here, 1, keepdims=False)
    inputs = [
        lax.dynamic_index_in_dim(saved_inputs[0], members[t], 0, keepdims=False) for t in (0, 1)
    ]
    halos = [
        jnp.concatenate(
            [
                from_behind(x[rows_here - BLOCK :], "mesh", 1),
                from_behind(x[:BLOCK], "mesh", -1),
            ],
            axis=0,
        )
        for x in inputs
    ]

    positions = jnp.arange(BLOCK)
    block_ids = jnp.arange(counts.shape[0])
    global_ids = part_here * blocks_here + jnp.arange(blocks_here)
    near_ids = jnp.stack([key_blocks[:, 1], global_ids, key_blocks[:, 0]], axis=1)
    near_counts = jnp.sum(
        jnp.where(block_ids[None, None, :] == near_ids[:, :, None], counts[None, None, :], 0),
        axis=2,
    )
    mask = jnp.where(positions[None, None, :] < near_counts[:, :, None], 0.0, -jnp.inf)
    mask = mask.reshape(blocks_here, 3 * BLOCK).astype(jnp.float32)

    def ready(t):
        normed = norm(inputs[t])[2]
        own = [project(normed, w) for w in (query_weight, key_weight, value_weight)]
        normed_halo = norm(halos[t])[2]
        near = [project(normed_halo, w) for w in (key_weight, value_weight)]
        return own + near + [mask, normed, normed_halo]

    upstream = pending[0]
    first = ready(0)
    second = ready(1)
    grad_attended = right_dot(upstream, out_weight).astype(jnp.bfloat16)
    att0, n0, nh0, gq, ko, vo, kh, vh = attention(*first, grad_attended)
    halo_term = (right_dot(kh, key_weight) + right_dot(vh, value_weight)).astype(jnp.bfloat16)
    from_after = from_behind(halo_term[:BLOCK], "mesh", -1)
    from_before = from_behind(halo_term[BLOCK:], "mesh", 1)
    att1, n1, nh1 = attention(*second)
    grad_normed = (
        right_dot(gq, query_weight) + right_dot(ko, key_weight) + right_dot(vo, value_weight)
    )
    middle = jnp.zeros((rows_here - 2 * BLOCK, features), jnp.bfloat16)
    grad_normed = grad_normed + jnp.concatenate([from_before, middle, from_after], axis=0).astype(
        jnp.float32
    )
    inv_rms, normed_float, _ = norm(inputs[0])
    grad_input = inv_rms * (
        grad_normed - normed_float * jnp.mean(grad_normed * normed_float, axis=-1, keepdims=True)
    )
    grad_x = (upstream.astype(jnp.float32) + grad_input).astype(jnp.bfloat16)
    passed = shifted(grad_x, "section", -1)
    later = jnp.where(section_here == sections - 1, top_grads[0], passed)
    layer_total, grad_x_last = last_tick(
        n0, nh0, n1, nh1, att0, att1, gq, ko, vo, kh, vh, upstream, later,
        *second[:6], inputs[1], query_weight, key_weight, value_weight, out_weight,
    )
    return (layer_total[None], jnp.stack([grad_x, grad_x_last])[:, None])


def solution(mesh):
    in_specs = (
        P("section", None, "mesh", None),
        P("section", None, None),
        P("section", None, None),
        P("section", None, None),
        P("section", None, None),
        P("section", "mesh", None),
        P(None, "mesh", None),
        P("mesh", None),
        P(),
        P(),
    )
    out_specs = (P("section", "mesh", None, None), P(None, "section", "mesh", None))
    return jax.shard_map(
        per_device, mesh=mesh, in_specs=in_specs, out_specs=out_specs, check_vma=False
    )
```

time: 226 us -> 214 us (0.947)
  Pallas kernels: 125 us -> 141 us
  other arithmetic: 19.3 us -> 7.35 us
  waiting for transfers between devices: 19 us -> 12.7 us
  local copies, waits for them, and re-layouts: 12.1 us -> 5.88 us
  starting transfers between devices: 19.6 us -> 16.9 us
    pallas_call x3, Pallas kernels: 125 us -> 141 us  [the longest x1 116 us: last_tick(): pl.pallas_call(functools.partial(last_kernel, count), out_shape=[jax.Shap...]
    dot_general x12 -> x6, matrix products: 14 us -> 7.48 us  [right_dot(): lax.dot_general(left, right, (((1,), (1,)), ((), ())), preferred_element_...]
    ppermute x6, waiting for transfers between devices: 19 us -> 12.7 us  [from_behind(): return lax.ppermute(value, axis, pairs)]
    convert_element_type x2 -> x0, local copies, waits for them, and re-layouts: 5.87 us -> none  [norm(): x_float = x.astype(jnp.float32)]
    dot_general x5 -> x10, matrix products: 11.4 us -> 17.2 us  [plain_dot(): return jnp.dot(left, right, preferred_element_type=jnp.float32)]
    convert_element_type x3 -> x0, other arithmetic: 4.62 us -> none  [the longest x2 4.28 us: norm(): x_float = x.astype(jnp.float32)]
    transpose x1 -> x0, other arithmetic: 4.27 us -> none  [per_device(): normed_own_t = normed.reshape(-1, features).T]
    ppermute x6, starting transfers between devices: 18.3 us -> 15.6 us  [from_behind(): return lax.ppermute(value, axis, pairs)]
  transfers between devices with their start and end apart: 7 -> 7, of which waited for: 6 -> 4; matrix products, arithmetic and copies ran while one was open for 12% -> 9% of each run, Pallas kernels for 0% -> 5%
where the time goes in v2:
time: 214 us
  Pallas kernels  141 us (66%)
  matrix products  24.7 us (12%)
  starting transfers between devices  16.9 us (8%)
  waiting for transfers between devices  12.7 us (6%)
  other arithmetic  7.35 us (3%)
  local copies, waits for them, and re-layouts  5.88 us (3%)
  between operations  4.83 us (2%)
    pallas_call x1, Pallas kernels, last_tick(): pl.pallas_call(functools.partial(last_kernel, count), out_shape=[jax.Shap...  116 us
    pallas_call x2, Pallas kernels, attention(): pl.pallas_call(functools.partial(forward_kernel if ga is None else both_k...  25.1 us
    dot_general x10, matrix products, plain_dot(): return jnp.dot(left, right, preferred_element_type=jnp.float32)  17.2 us
    ppermute x6, starting transfers between devices, from_behind(): return lax.ppermute(value, axis, pairs)  15.6 us
    ppermute x6, waiting for transfers between devices, from_behind(): return lax.ppermute(value, axis, pairs)  12.7 us
    dot_general x6, matrix products, right_dot(): lax.dot_general(left, right, (((1,), (1,)), ((), ())), preferred_element_...  7.48 us
  transfers between devices with their start and end apart: 7, of which 4 were waited for; matrix products, arithmetic and copies ran while one was open for 9% of the time, Pallas kernels for 5%

profile of v2, /device:TPU:0, one launch (start us, length us, event | category | flops | bytes accessed | tf_op | source)
XLA Modules:
  0.0 213.6 jit_solution(2323475098513109473)
XLA Ops:
  0.6 0.0 copy-start
  0.6 0.0 copy-start.1
  0.7 0.6 copy-done
  1.3 0.1 constant_dynamic-slice_fusion
  1.4 0.5 fusion.48
  5.8 2.1 dynamic-slice_bitcast_fusion.2
  7.9 2.9 %collective-permute-start.2 = (bf16[128,1024]{1,0:T(8,128)(2,1)}, bf16[128,1024]{1,0:T(8,128)(2,1)S(1)}, u32[]{:S(2)}, u32[]{:S(2)}) collective-permute-start(bf16[128,1024]{1,0:T(8,128)(2,1)} %get-tuple-element.37), channel_id=1, source_target_pairs={{0,1},{1,2},{2,3},{3,4},{4,5},{5,6},{6,7},{7,8},{8,9},{9,10},{10,1... | collective-permute-start | bytes 786440 | tf_op jit(solution)/shard_map/ppermute | solution.py:21
  10.8 4.0 %collective-permute-start.3 = (bf16[128,1024]{1,0:T(8,128)(2,1)S(1)}, bf16[128,1024]{1,0:T(8,128)(2,1)S(1)}, u32[]{:S(2)}, u32[]{:S(2)}) collective-permute-start(bf16[128,1024]{1,0:T(8,128)(2,1)S(1)} %get-tuple-element.38), channel_id=1, source_target_pairs={{0,15},{1,0},{2,1},{3,2},{4,3},{5,4},{6,5},{7,6},{8,7},{9,8},{10,9... | collective-permute-start | bytes 786440 | tf_op jit(solution)/shard_map/ppermute | solution.py:21
  14.8 2.0 collective-permute-start.1
  16.9 0.0 collective-permute-start
  16.9 0.2 fusion.11
  17.1 0.1 fusion.49
  17.1 0.1 pad_add_fusion
  17.2 0.1 copy.14
  17.3 0.2 fusion.21
  17.5 0.1 copy.15
  17.6 0.1 broadcast_bitcast_fusion
  17.7 3.3 %convolution_convert_fusion.9.ko = bf16[256,1024]{1,0:T(8,128)(2,1)} fusion(bf16[1,1024,1024]{2,1,0:T(8,128)(2,1)} %param.12, f32[256]{0:T(256)S(1)} %add_rsqrt_fusion.3, bf16[1,3,256,1024]{3,2,1,0:T(8,128)(2,1)S(1)} %copy-done.1, s32[]{:T(128)S(6)} %select_n.29), kind=kOutput, calls=%fused_computation.25 | convolution fusion | flops 537919488 | bytes 3146756 | tf_op jit(solution)/shard_map/dot_general | solution.py:43
  21.0 1.5 convolution_convert_fusion.8.vo
  22.6 0.0 copy-done.8
  22.6 1.5 convolution_convert_fusion.10.q
  24.1 0.3 copy-done.21
  24.4 1.6 convolution_convert_fusion.5.ga
  26.0 0.6 compare_select_fusion.mask
  26.6 0.9 fusion.4.no
  27.5 3.4 %collective-permute-done.1 = bf16[128,1024]{1,0:T(8,128)(2,1)S(1)} collective-permute-done((bf16[128,1024]{1,0:T(8,128)(2,1)}, bf16[128,1024]{1,0:T(8,128)(2,1)S(1)}, u32[]{:S(2)}, u32[]{:S(2)}) %collective-permute-start.1) | collective-permute-done | bytes 262176 | tf_op jit(solution)/shard_map/ppermute | solution.py:21
  30.9 2.6 %collective-permute-done = bf16[128,1024]{1,0:T(8,128)(2,1)S(1)} collective-permute-done((bf16[128,1024]{1,0:T(8,128)(2,1)}, bf16[128,1024]{1,0:T(8,128)(2,1)S(1)}, u32[]{:S(2)}, u32[]{:S(2)}) %collective-permute-start) | collective-permute-done | bytes 262176 | tf_op jit(solution)/shard_map/ppermute | solution.py:21
  33.6 0.2 fusion.13
  33.8 0.0 copy-start.2
  33.8 0.2 fusion.14.nh
  33.9 1.5 convolution_convert_fusion.6.vh
  35.5 0.1 copy-done.2
  35.5 1.5 convolution_convert_fusion.7.kh
  37.1 0.0 collective-permute-done.2
  37.1 0.2 fusion.17
  37.3 0.2 fusion.18.nh
  37.4 1.5 convolution_convert_fusion.vh.value_halo1
  39.0 15.0 %attention_both_ways.1 = (bf16[1024,256]{1,0:T(8,128)(2,1)}, bf16[1024,256]{1,0:T(8,128)(2,1)}, bf16[1024,256]{1,0:T(8,128)(2,1)}, bf16[256,1024]{1,0:T(8,128)(2...) custom-call(bf16[256,1024]{1,0:T(8,128)(2,1)} %convolution_convert_f, ...), custom_call_target="tpu_custom_call" | custom-call | flops 1207959552 | bytes 6291456 | tf_op jit(solution)/shard_map/attention_both_ways/pallas_call | solution.py:155
  54.0 0.0 copy-start.3
  54.0 2.6 %fusion.37 = f32[256,1024]{1,0:T(8,128)S(1)} fusion(bf16[256,1024]{1,0:T(8,128)(2,1)} %get-tuple-element.21.gq0, bf16[1,1024,1024]{2,1,0:T(8,128)(2,1)} %param.11), kind=kOutput, calls=%fused_computation.83 | convolution fusion | flops 536870912 | bytes 3670016 | tf_op jit(solution)/shard_map/dot_general | solution.py:31
  56.7 0.0 copy-start.6
  56.7 0.8 fusion.30
  57.5 0.7 copy-done.6
  58.3 0.1 copy-done.18
  58.4 0.7 fusion.5
  59.2 2.4 %collective-permute-start.4 = (bf16[128,1024]{1,0:T(8,128)(2,1)S(1)}, bf16[128,1024]{1,0:T(8,128)(2,1)S(1)}, u32[]{:S(2)}, u32[]{:S(2)}) collective-permute-start(bf16[128,1024]{1,0:T(8,128)(2,1)S(1)} %get-tuple-element.41), channel_id=1, source_target_pairs={{0,1},{1,2},{2,3},{3,4},{4,5},{5,6},{6,7},{7,8},{8,9},{9,10},{10,1... | collective-permute-start | bytes 786440 | tf_op jit(solution)/shard_map/ppermute | solution.py:21
  61.6 4.2 %collective-permute-start.5 = (bf16[128,1024]{1,0:T(8,128)(2,1)S(1)}, bf16[128,1024]{1,0:T(8,128)(2,1)S(1)}, u32[]{:S(2)}, u32[]{:S(2)}) collective-permute-start(bf16[128,1024]{1,0:T(8,128)(2,1)S(1)} %get-tuple-element.42), channel_id=1, source_target_pairs={{0,15},{1,0},{2,1},{3,2},{4,3},{5,4},{6,5},{7,6},{8,7},{9,8},{10,9... | collective-permute-start | bytes 786440 | tf_op jit(solution)/shard_map/ppermute | solution.py:21
  65.8 0.7 convolution_add_fusion.2
  66.6 1.5 convolution_convert_fusion.1.kh.key_halo1
  68.1 3.8 %collective-permute-done.4 = bf16[128,1024]{1,0:T(8,128)(2,1)S(1)} collective-permute-done((bf16[128,1024]{1,0:T(8,128)(2,1)S(1)}, bf16[128,1024]{1,0:T(8,128)(2,1)S(1)}, u32[]{:S(2)}, u32[]{:S(2)}) %collective-permute-start.4) | collective-permute-done | bytes 262176 | tf_op jit(solution)/shard_map/ppermute | solution.py:21
  71.9 2.8 %collective-permute-done.5 = bf16[128,1024]{1,0:T(8,128)(2,1)S(1)} collective-permute-done((bf16[128,1024]{1,0:T(8,128)(2,1)S(1)}, bf16[128,1024]{1,0:T(8,128)(2,1)S(1)}, u32[]{:S(2)}, u32[]{:S(2)}) %collective-permute-start.5) | collective-permute-done | bytes 262176 | tf_op jit(solution)/shard_map/ppermute | solution.py:21
  74.7 1.0 fusion.6
  75.8 0.5 fusion.15
  76.3 1.6 convolution_convert_fusion.3.ko.key1
  77.9 1.6 convolution_convert_fusion.2.vo.value1
  79.5 1.3 collective-permute-start.6
  80.8 0.9 fusion.16.no
  81.7 1.5 convolution_convert_fusion.4.q.q1
  83.3 10.0 %attention_forward.1 = (bf16[1024,256]{1,0:T(8,128)(2,1)}, bf16[1024,256]{1,0:T(8,128)(2,1)}, bf16[1024,256]{1,0:T(8,128)(2,1)}) custom-call(bf16[256,1024]{1,0:T(8,128)(2,1)} %convolution_convert_fusion.4.q.q1, bf16[256,1024]{1,0:T(8,128)(2,1)} %convolution_convert_fusion.3.ko.key1, bf16[256,1024]{1,0:T(8,128)(2,1)} %convolution_convert_fusion.2.vo.value1, ...), custom_call_target="tpu_custom_call" | custom-call | flops 402653184 | bytes 6291456 | tf_op jit(solution)/shard_map/attention_forward/pallas_call | solution.py:155
  93.3 0.0 collective-permute-done.6
  93.3 0.9 bitcast_select_fusion.up1
  94.2 116.2 %last_tick.1 = (f32[64,4,1024]{2,1,0:T(4,128)}, bf16[256,1024]{1,0:T(8,128)(2,1)}) custom-call(bf16[1024,256]{1,0:T(8,128)(2,1)} %get-tuple-element.15.n0, bf16[1024,256]{1,0:T(8,128)(2,1)} %get-tuple-element.16.nh0, bf16[1024,256]{1,0:T(8,128)(2,1)} %get-tuple-element.17.n1, bf16[1024,256]{1,0:T(8,128)(2,1)} %get-tuple-element.18.nh1, ...), custom_call_target="tpu_custom_call" | custom-call | flops 6442450944 | bytes 209715200 | tf_op jit(solution)/shard_map/last_tick/pallas_call | solution.py:355
  210.4 2.2 %maximum_bitcast_fusion = bf16[2,1,256,1024]{3,2,1,0:T(8,128)(2,1)} fusion(bf16[1,256,1024]{2,1,0:T(8,128)(2,1)} %bitcast.119, bf16[1,256,1024]{2,1,0:T(8,128)(2,1)S(1)} %bitcast.116), kind=kLoop, calls=%fused_computation.41 | loop fusion | flops 524288 | bytes 2097152
  212.6 1.0 copy.20
  (41 shorter events, 0.1 us)
Async XLA Ops:
  0.6 0.7 copy-start
  0.6 16.2 %copy-start.1 = (bf16[1,3,256,1024]{3,2,1,0:T(8,128)(2,1)S(1)}, bf16[1,3,256,1024]{3,2,1,0:T(8,128)(2,1)}, u32[]{:S(2)}) copy-start(bf16[1,3,256,1024]{3,2,1,0:T(8,128)(2,1)} %param.10) | copy-start | bytes 4718596
  0.7 16.4 %copy-start.19 = (s32[2,2]{1,0:T(2,128)S(1)}, s32[2,2]{1,0:T(2,128)}, u32[]{:S(2)}) copy-start(s32[2,2]{1,0:T(2,128)} %param.17) | copy-start | bytes 52
  0.7 16.7 %copy-start.20 = (s32[32]{0:T(128)S(1)}, s32[32]{0:T(128)}, u32[]{:S(2)}) copy-start(s32[32]{0:T(128)} %param.18) | copy-start | bytes 388
  7.9 29.2 %collective-permute-start.2 = (bf16[128,1024]{1,0:T(8,128)(2,1)}, bf16[128,1024]{1,0:T(8,128)(2,1)S(1)}, u32[]{:S(2)}, u32[]{:S(2)}) collective-permute-start(bf16[128,1024]{1,0:T(8,128)(2,1)} %get-tuple-element.37), channel_id=1, source_target_pairs={{0,1},{1,2},{2,3},{3,4},{4,5},{5,6},{6,7},{7,8},{8,9},{9,10},{10,1... | collective-permute-start | bytes 786440 | tf_op jit(solution)/shard_map/ppermute | solution.py:21
  10.8 26.2 %collective-permute-start.3 = (bf16[128,1024]{1,0:T(8,128)(2,1)S(1)}, bf16[128,1024]{1,0:T(8,128)(2,1)S(1)}, u32[]{:S(2)}, u32[]{:S(2)}) collective-permute-start(bf16[128,1024]{1,0:T(8,128)(2,1)S(1)} %get-tuple-element.38), channel_id=1, source_target_pairs={{0,15},{1,0},{2,1},{3,2},{4,3},{5,4},{6,5},{7,6},{8,7},{9,8},{10,9... | collective-permute-start | bytes 786440 | tf_op jit(solution)/shard_map/ppermute | solution.py:21
  14.8 16.1 %collective-permute-start.1 = (bf16[128,1024]{1,0:T(8,128)(2,1)}, bf16[128,1024]{1,0:T(8,128)(2,1)S(1)}, u32[]{:S(2)}, u32[]{:S(2)}) collective-permute-start(bf16[128,1024]{1,0:T(8,128)(2,1)} %get-tuple-element.39), channel_id=1, source_target_pairs={{0,15},{1,0},{2,1},{3,2},{4,3},{5,4},{6,5},{7,6},{8,7},{9,8},{10,9... | collective-permute-start | bytes 786440 | tf_op jit(solution)/shard_map/ppermute | solution.py:21
  16.9 16.7 %collective-permute-start = (bf16[128,1024]{1,0:T(8,128)(2,1)}, bf16[128,1024]{1,0:T(8,128)(2,1)S(1)}, u32[]{:S(2)}, u32[]{:S(2)}) collective-permute-start(bf16[128,1024]{1,0:T(8,128)(2,1)} %get-tuple-element.40), channel_id=1, source_target_pairs={{0,1},{1,2},{2,3},{3,4},{4,5},{5,6},{6,7},{7,8},{8,9},{9,10},{10,1... | collective-permute-start | bytes 786440 | tf_op jit(solution)/shard_map/ppermute | solution.py:21
  17.6 3.4 %copy-start.4 = (bf16[1,1024,1024]{2,1,0:T(8,128)(2,1)S(1)}, bf16[1,1024,1024]{2,1,0:T(8,128)(2,1)}, u32[]{:S(2)}) copy-start(bf16[1,1024,1024]{2,1,0:T(8,128)(2,1)} %param.13) | copy-start | bytes 6291460
  21.0 1.6 copy-start.8
  22.6 1.6 copy-start.12
  22.6 1.8 copy-start.21
  26.6 7.4 %copy-start.5 = (bf16[1,1024,1024]{2,1,0:T(8,128)(2,1)S(1)}, bf16[1,1024,1024]{2,1,0:T(8,128)(2,1)}, u32[]{:S(2)}) copy-start(bf16[1,1024,1024]{2,1,0:T(8,128)(2,1)} %param.13) | copy-start | bytes 6291460
  33.8 1.8 copy-start.2
  33.9 3.1 %copy-start.15 = (bf16[256,1024]{1,0:T(8,128)(2,1)}, bf16[256,1024]{1,0:T(8,128)(2,1)S(1)}, u32[]{:S(2)}) copy-start(bf16[256,1024]{1,0:T(8,128)(2,1)S(1)} %fusion.14.nh) | copy-start | bytes 1572868
  37.4 29.2 %copy-start.10 = (bf16[256,1024]{1,0:T(8,128)(2,1)}, bf16[256,1024]{1,0:T(8,128)(2,1)S(1)}, u32[]{:S(2)}) copy-start(bf16[256,1024]{1,0:T(8,128)(2,1)S(1)} %fusion.18.nh) | copy-start | bytes 1572868
  54.0 2.7 %copy-start.3 = (bf16[1,1024,1024]{2,1,0:T(8,128)(2,1)S(1)}, bf16[1,1024,1024]{2,1,0:T(8,128)(2,1)}, u32[]{:S(2)}) copy-start(bf16[1,1024,1024]{2,1,0:T(8,128)(2,1)} %param.12) | copy-start | bytes 6291460
  54.0 2.7 %copy-start.14 = (bf16[256,1024]{1,0:T(8,128)(2,1)S(1)}, bf16[256,1024]{1,0:T(8,128)(2,1)}, u32[]{:S(2)}) copy-start(bf16[256,1024]{1,0:T(8,128)(2,1)} %get-tuple-element.24.kh0) | copy-start | bytes 1572868
  56.7 1.6 copy-start.6
  56.7 1.7 copy-start.18
  58.4 7.5 %copy-start.13 = (bf16[256,1024]{1,0:T(8,128)(2,1)S(1)}, bf16[256,1024]{1,0:T(8,128)(2,1)}, u32[]{:S(2)}) copy-start(bf16[256,1024]{1,0:T(8,128)(2,1)} %get-tuple-element.22.ko0) | copy-start | bytes 1572868
  59.2 12.7 %collective-permute-start.4 = (bf16[128,1024]{1,0:T(8,128)(2,1)S(1)}, bf16[128,1024]{1,0:T(8,128)(2,1)S(1)}, u32[]{:S(2)}, u32[]{:S(2)}) collective-permute-start(bf16[128,1024]{1,0:T(8,128)(2,1)S(1)} %get-tuple-element.41), channel_id=1, source_target_pairs={{0,1},{1,2},{2,3},{3,4},{4,5},{5,6},{6,7},{7,8},{8,9},{9,10},{10,1... | collective-permute-start | bytes 786440 | tf_op jit(solution)/shard_map/ppermute | solution.py:21
  61.6 13.2 %collective-permute-start.5 = (bf16[128,1024]{1,0:T(8,128)(2,1)S(1)}, bf16[128,1024]{1,0:T(8,128)(2,1)S(1)}, u32[]{:S(2)}, u32[]{:S(2)}) collective-permute-start(bf16[128,1024]{1,0:T(8,128)(2,1)S(1)} %get-tuple-element.42), channel_id=1, source_target_pairs={{0,15},{1,0},{2,1},{3,2},{4,3},{5,4},{6,5},{7,6},{8,7},{9,8},{10,9... | collective-permute-start | bytes 786440 | tf_op jit(solution)/shard_map/ppermute | solution.py:21
  66.6 8.1 %copy-start.17 = (bf16[256,1024]{1,0:T(8,128)(2,1)S(1)}, bf16[256,1024]{1,0:T(8,128)(2,1)}, u32[]{:S(2)}) copy-start(bf16[256,1024]{1,0:T(8,128)(2,1)} %get-tuple-element.23.vo0) | copy-start | bytes 1572868
  76.3 4.5 %copy-start.7 = (bf16[256,1024]{1,0:T(8,128)(2,1)}, bf16[256,1024]{1,0:T(8,128)(2,1)S(1)}, u32[]{:S(2)}) copy-start(bf16[256,1024]{1,0:T(8,128)(2,1)S(1)} %get-tuple-element.35.x1) | copy-start | bytes 1572868
  77.9 3.8 %copy-start.9 = (bf16[1,1024,1024]{2,1,0:T(8,128)(2,1)S(1)}, bf16[1,1024,1024]{2,1,0:T(8,128)(2,1)}, u32[]{:S(2)}) copy-start(bf16[1,1024,1024]{2,1,0:T(8,128)(2,1)} %param.11) | copy-start | bytes 6291460
  79.5 13.8 %collective-permute-start.6 = (bf16[256,1024]{1,0:T(8,128)(2,1)S(1)}, bf16[256,1024]{1,0:T(8,128)(2,1)S(1)}, u32[]{:S(2)}, u32[]{:S(2)}) collective-permute-start(bf16[256,1024]{1,0:T(8,128)(2,1)S(1)} %get-tuple-element.36), channel_id=1, source_target_pairs={{16,0},{17,1},{18,2},{19,3},{20,4},{21,5},{22,6},{23,7},{24,8},{25... | collective-permute-start | bytes 1572872 | tf_op jit(solution)/shard_map/ppermute | solution.py:27
  83.3 10.0 %copy-start.16 = (bf16[1,256,1024]{2,1,0:T(8,128)(2,1)S(1)}, bf16[1,256,1024]{2,1,0:T(8,128)(2,1)}, u32[]{:S(2)}) copy-start(bf16[1,256,1024]{2,1,0:T(8,128)(2,1)} %param.16) | copy-start | bytes 1572868
  210.4 2.2 %copy-start.11 = (f32[64,4,1024]{2,1,0:T(4,128)S(1)}, f32[64,4,1024]{2,1,0:T(4,128)}, u32[]{:S(2)}) copy-start(f32[64,4,1024]{2,1,0:T(4,128)} %get-tuple-element.26) | copy-start | bytes 3145732

commit v3 on v2

--- a/solution.py
+++ b/solution.py
@@ -10,6 +10,7 @@
 
 HEADS = 8
 BLOCK = 128
+GROUP = 2
 OFFSETS = (1, -1)
 EPSILON = 1e-06
 MESH = pl.DeviceIdType.MESH
@@ -52,18 +53,17 @@
 def softmax(q, k, mask, scale):
     scores = right_dot(q, k) * scale + mask
     raised = jnp.exp(scores - jnp.max(scores, axis=-1, keepdims=True))
-    return raised / jnp.sum(raised, axis=-1, keepdims=True)
-
-
-def head_forward(scale, q_ref, ko_ref, vo_ref, kh_ref, vh_ref, mask_ref, att_ref):
-    every = slice(None)
-    keys = near_keys(ko_ref, kh_ref, every)
-    values = near_keys(vo_ref, vh_ref, every)
+    return raised * (1.0 / jnp.sum(raised, axis=-1, keepdims=True))
+
+
+def head_forward(scale, columns, q_ref, ko_ref, vo_ref, kh_ref, vh_ref, mask_ref, att_ref):
+    keys = near_keys(ko_ref, kh_ref, columns)
+    values = near_keys(vo_ref, vh_ref, columns)
     for b in range(q_ref.shape[0] // BLOCK):
         rows = slice(b * BLOCK, (b + 1) * BLOCK)
         near = slice(b * BLOCK, (b + 3) * BLOCK)
-        probs = softmax(q_ref[rows], keys[near], mask_ref[b : b + 1, :], scale)
-        att_ref[:, rows] = lax.dot_general(
+        probs = softmax(q_ref[rows, columns], keys[near], mask_ref[b : b + 1, :], scale)
+        att_ref[columns, rows] = lax.dot_general(
             values[near], probs.astype(jnp.bfloat16), (((0,), (1,)), ((), ())),
             preferred_element_type=jnp.float32,
         ).astype(jnp.bfloat16)
@@ -89,7 +89,7 @@
         probs = softmax(q, k, mask_ref[b : b + 1, :], scale)
         probs_bf = probs.astype(jnp.bfloat16)
         if att_ref is not None:
-            att_ref[:, rows] = lax.dot_general(
+            att_ref[columns, rows] = lax.dot_general(
                 v, probs_bf, (((0,), (1,)), ((), ())), preferred_element_type=jnp.float32
             ).astype(jnp.bfloat16)
         grad_probs = right_dot(ga, v)
@@ -118,8 +118,14 @@
     to_ref[...] = left_dot(from_ref[...], identity).astype(jnp.bfloat16)
 
 
+def heads_of(q, scale):
+    dim = round(1.0 / scale**2)
+    return [slice(first, first + dim) for first in range(0, q.shape[1], dim)]
+
+
 def forward_kernel(scale, q, ko, vo, kh, vh, mask, no, nh, att, not_, nht):
-    head_forward(scale, q, ko, vo, kh, vh, mask, att)
+    for columns in heads_of(q, scale):
+        head_forward(scale, columns, q, ko, vo, kh, vh, mask, att)
     turn(no, not_)
     turn(nh, nht)
 
@@ -127,9 +133,8 @@
 def both_kernel(
     scale, q, ko, vo, kh, vh, mask, no, nh, ga, att, not_, nht, gq, kto, vto, kth, vth
 ):
-    head_backward(
-        scale, slice(None), q, ko, vo, kh, vh, ga, mask, gq, kto, vto, kth, vth, att
-    )
+    for columns in heads_of(q, scale):
+        head_backward(scale, columns, q, ko, vo, kh, vh, ga, mask, gq, kto, vto, kth, vth, att)
     turn(no, not_)
     turn(nh, nht)
 
@@ -138,8 +143,8 @@
     rows, features = q.shape
     dim = features // HEADS
     halo = kh.shape[0]
-    flat = lambda n: pl.BlockSpec((n, dim), lambda h: (0, h))
-    tall = lambda n: pl.BlockSpec((dim, n), lambda h: (h, 0))
+    flat = lambda n: pl.BlockSpec((n, GROUP * dim), lambda h: (0, h))
+    tall = lambda n: pl.BlockSpec((GROUP * dim, n), lambda h: (h, 0))
     shape = lambda n: jax.ShapeDtypeStruct((n, features), jnp.bfloat16)
     tall_shape = lambda n: jax.ShapeDtypeStruct((features, n), jnp.bfloat16)
     in_specs = [flat(rows), flat(rows), flat(rows), flat(halo), flat(halo)]
@@ -156,7 +161,7 @@
         functools.partial(
             forward_kernel if ga is None else both_kernel, 1.0 / math.sqrt(dim)
         ),
-        grid=(HEADS,),
+        grid=(HEADS // GROUP,),
         in_specs=in_specs,
         out_specs=out_specs,
         out_shape=out_shape,
@@ -180,11 +185,12 @@
     (projection, quarter, quarter % 2) for projection in range(3) for quarter in range(QUARTERS)
 )
 EARLY = 4
+LAG = 2
 
 
 def last_kernel(
     count, n0, nh0, n1, nh1, att0, att1, gq0, ko0, vo0, kh0, vh0, up0, up1,
-    q1, key1, value1, key_halo1, value_halo1, mask, x1, wq, wk, wv, wo,
+    q1, key1, value1, key_halo1, value_halo1, mask, x1, wq, wk, wv, wo, grad_x0,
     out_ref, grad_x_ref,
     nlhs, alhs, keep, send, recv, ga1, gq1, ko1, vo1, kh1, vh1, term, term_in,
     send_sem, recv_sem, term_send, term_recv,
@@ -283,13 +289,42 @@
     ga1[...] = right_dot(up1[...], wo[...]).astype(jnp.bfloat16)
     dim = features // HEADS
 
-    @pl.loop(0, HEADS)
-    def _(h):
-        columns = pl.ds(pl.multiple_of(h * dim, dim), dim)
-        head_backward(
-            scale, columns, q1, key1, value1, key_halo1, value_halo1, ga1, mask,
-            gq1, ko1, vo1, kh1, vh1,
-        )
+    def heads(first, last):
+        @pl.loop(first, last)
+        def _(pair):
+            for h in range(GROUP):
+                columns = pl.ds(pl.multiple_of((pair * GROUP + h) * dim, dim), dim)
+                head_backward(
+                    scale, columns, q1, key1, value1, key_halo1, value_halo1, ga1, mask,
+                    gq1, ko1, vo1, kh1, vh1,
+                )
+
+    def advance(p, k):
+        portion = PORTIONS[p]
+        size = features >> (k + 1)
+        if k == 0:
+            keep[p] = product(portion, slice(0, middle))
+        copy_of(p, k).wait_recv()
+        if k + 1 < bits:
+            left = size // 2
+            send[p, starts[k + 1] : starts[k + 1] + left] = (
+                keep[p, left:size]
+                + recv[p, starts[k] + left : starts[k] + size].astype(jnp.float32)
+            ).astype(jnp.bfloat16)
+            copy_of(p, k + 1).start()
+            keep[p, :left] += recv[p, starts[k] : starts[k] + left].astype(jnp.float32)
+        else:
+            out_ref[:, portion[0], columns_of(portion)] = keep[p, :size] + recv[
+                p, starts[k] : starts[k] + size
+            ].astype(jnp.float32)
+
+    groups = HEADS // GROUP
+    done = 0
+    for k, last in enumerate((groups // 2, 3 * groups // 4, groups)):
+        heads(done, last)
+        done = last
+        for p in range(EARLY):
+            advance(p, k)
 
     term[...] = (right_dot(kh1[...], wk[...]) + right_dot(vh1[...], wv[...])).astype(jnp.bfloat16)
     for side in (0, 1):
@@ -298,9 +333,6 @@
         arrange(nlhs, slot, orders[slot], (n0, n1, nh0, nh1))
     for p in range(EARLY, len(PORTIONS)):
         begin(p)
-    for p, portion in enumerate(PORTIONS):
-        keep[p] = product(portion, slice(0, middle))
-
     def finish_input():
         x_float = x1[...].astype(jnp.float32)
         inv_rms = lax.rsqrt(jnp.mean(x_float * x_float, axis=-1, keepdims=True) + EPSILON)
@@ -315,25 +347,19 @@
         pieces.append(term_in[BLOCK:].astype(jnp.float32))
         grad = grad + jnp.concatenate(pieces, axis=0)
         grad = inv_rms * (grad - normed * jnp.mean(grad * normed, axis=-1, keepdims=True))
-        grad_x_ref[...] = (up1[...].astype(jnp.float32) + grad).astype(jnp.bfloat16)
-
-    for k in range(bits):
-        size = features >> (k + 1)
-        for p, portion in enumerate(PORTIONS):
-            copy_of(p, k).wait_recv()
-            if k + 1 < bits:
-                left = size // 2
-                send[p, starts[k + 1] : starts[k + 1] + left] = (
-                    keep[p, left:size]
-                    + recv[p, starts[k] + left : starts[k] + size].astype(jnp.float32)
-                ).astype(jnp.bfloat16)
-                copy_of(p, k + 1).start()
-                keep[p, :left] += recv[p, starts[k] : starts[k] + left].astype(jnp.float32)
-            else:
-                out_ref[:, portion[0], columns_of(portion)] = keep[p, :size] + recv[
-                    p, starts[k] : starts[k] + size
-                ].astype(jnp.float32)
-        if k == 0:
+        grad_x_ref[0] = grad_x0[...]
+        grad_x_ref[1] = (up1[...].astype(jnp.float32) + grad).astype(jnp.bfloat16)
+
+    for p in range(EARLY):
+        for k in range(3, bits):
+            advance(p, k)
+    rest = range(EARLY, len(PORTIONS))
+    for stage in range(len(rest) + LAG * (bits - 1)):
+        for k in reversed(range(bits)):
+            place = stage - LAG * k
+            if 0 <= place < len(rest):
+                advance(rest[place], k)
+        if stage == LAG:
             finish_input()
     for k in range(bits):
         for p in range(len(PORTIONS)):
@@ -356,7 +382,7 @@
         functools.partial(last_kernel, count),
         out_shape=[
             jax.ShapeDtypeStruct((chunk, 4, features), jnp.float32),
-            jax.ShapeDtypeStruct((rows, features), jnp.bfloat16),
+            jax.ShapeDtypeStruct((2, rows, features), jnp.bfloat16),
         ],
         in_specs=[pl.BlockSpec(memory_space=pltpu.VMEM)] * len(operands),
         out_specs=[pl.BlockSpec(memory_space=pltpu.VMEM)] * 2,
@@ -449,13 +475,15 @@
 
     upstream = pending[0]
     first = ready(0)
-    second = ready(1)
     grad_attended = right_dot(upstream, out_weight).astype(jnp.bfloat16)
     att0, n0, nh0, gq, ko, vo, kh, vh = attention(*first, grad_attended)
     halo_term = (right_dot(kh, key_weight) + right_dot(vh, value_weight)).astype(jnp.bfloat16)
+    halo_term, halos[1] = lax.optimization_barrier((halo_term, halos[1]))
     from_after = from_behind(halo_term[:BLOCK], "mesh", -1)
     from_before = from_behind(halo_term[BLOCK:], "mesh", 1)
+    second = ready(1)
     att1, n1, nh1 = attention(*second)
+    from_after, from_before, att1 = lax.optimization_barrier((from_after, from_before, att1))
     grad_normed = (
         right_dot(gq, query_weight) + right_dot(ko, key_weight) + right_dot(vo, value_weight)
     )
@@ -470,11 +498,11 @@
     grad_x = (upstream.astype(jnp.float32) + grad_input).astype(jnp.bfloat16)
     passed = shifted(grad_x, "section", -1)
     later = jnp.where(section_here == sections - 1, top_grads[0], passed)
-    layer_total, grad_x_last = last_tick(
+    layer_total, input_grads = last_tick(
         n0, nh0, n1, nh1, att0, att1, gq, ko, vo, kh, vh, upstream, later,
-        *second[:6], inputs[1], query_weight, key_weight, value_weight, out_weight,
-    )
-    return (layer_total[None], jnp.stack([grad_x, grad_x_last])[:, None])
+        *second[:6], inputs[1], query_weight, key_weight, value_weight, out_weight, grad_x,
+    )
+    return (layer_total[None], input_grads[:, None])
 
 
 def solution(mesh):

time: 214 us -> 211 us (0.986)
  waiting for transfers between devices: 12.7 us -> 3.09 us
  Pallas kernels: 141 us -> 144 us
  local copies, waits for them, and re-layouts: 5.88 us -> 8.38 us
  matrix products: 24.7 us -> 27.2 us
    ppermute x6, waiting for transfers between devices: 12.7 us -> 0.59 us  [from_behind(): return lax.ppermute(value, axis, pairs)]
    dot_general x6, matrix products: 7.48 us -> 11.8 us  [right_dot(): lax.dot_general(left, right, (((1,), (1,)), ((), ())), preferred_element_...]
    pallas_call x1, Pallas kernels: 116 us -> 120 us  [last_tick(): pl.pallas_call(functools.partial(last_kernel, count), out_shape=[jax.Shap...]
    ppermute x1, waiting for transfers between devices: 0.01 us -> 2.5 us  [shifted(): return lax.ppermute(x, axis, pairs)]
    unnamed x1 -> x0, other arithmetic: 2.2 us -> none
    unnamed x46 -> x53, local copies, waits for them, and re-layouts: 2.96 us -> 4.51 us
  transfers between devices with their start and end apart: 7 -> 7, of which waited for: 4 -> 2; matrix products, arithmetic and copies ran while one was open for 9% -> 12% of each run, Pallas kernels for 5% -> 11%
where the time goes in v3:
time: 211 us
  Pallas kernels  144 us (68%)
  matrix products  27.2 us (13%)
  starting transfers between devices  16.6 us (8%)
  local copies, waits for them, and re-layouts  8.38 us (4%)
  other arithmetic  6.14 us (3%)
  between operations  4.88 us (2%)
  waiting for transfers between devices  3.09 us (1%)
    pallas_call x1, Pallas kernels, last_tick(): pl.pallas_call(functools.partial(last_kernel, count), out_shape=[jax.Shap...  120 us
    pallas_call x2, Pallas kernels, attention(): pl.pallas_call(functools.partial(forward_kernel if ga is None else both_k...  23.9 us
    dot_general x10, matrix products, plain_dot(): return jnp.dot(left, right, preferred_element_type=jnp.float32)  15.4 us
    ppermute x6, starting transfers between devices, from_behind(): return lax.ppermute(value, axis, pairs)  15.3 us
    dot_general x6, matrix products, right_dot(): lax.dot_general(left, right, (((1,), (1,)), ((), ())), preferred_element_...  11.8 us
    unnamed x53, local copies, waits for them, and re-layouts  4.51 us
  transfers between devices with their start and end apart: 7, of which 2 were waited for; matrix products, arithmetic and copies ran while one was open for 12% of the time, Pallas kernels for 11%

profile of v3, /device:TPU:0, one launch (start us, length us, event | category | flops | bytes accessed | tf_op | source)
XLA Modules:
  0.0 210.5 jit_solution(14372637613663076591)
XLA Ops:
  0.6 0.0 copy-start
  0.6 0.0 copy-start.1
  0.7 0.7 copy-done
  1.3 0.1 constant_dynamic-slice_fusion
  1.4 0.5 fusion.49
  5.8 0.0 copy-start.2
  5.8 2.3 %dynamic-slice_bitcast_fusion.2 = (bf16[128,1024]{1,0:T(8,128)(2,1)}, bf16[128,1024]{1,0:T(8,128)(2,1)S(1)}, bf16[128,1024]{1,0:T(8,128)(2,1)}, bf16[128,1024]{1,0:T(8,128)(2,1)}) fusion(bf16[1,3,256,1024]{3,2,1,0:T(8,128)(2,1)} %param.10, s32[]{:T(128)S(6)} %select_n.32, s32[]{:T(128)S(6)} %add.88, s32[]{:T(128)S(6)} %select_n.29), kind=kLoop, calls=%fused_computation.50 | loop fusion | bytes 2097164 | tf_op jit(solution)/shard_map/slice | solution.py:450
  8.1 2.9 %collective-permute-start.2 = (bf16[128,1024]{1,0:T(8,128)(2,1)}, bf16[128,1024]{1,0:T(8,128)(2,1)}, u32[]{:S(2)}, u32[]{:S(2)}) collective-permute-start(bf16[128,1024]{1,0:T(8,128)(2,1)} %get-tuple-element.46), channel_id=1, source_target_pairs={{0,1},{1,2},{2,3},{3,4},{4,5},{5,6},{6,7},{7,8},{8,9},{9,10},{10,1... | collective-permute-start | bytes 786440 | tf_op jit(solution)/shard_map/ppermute | solution.py:22
  11.0 4.0 %collective-permute-start.3 = (bf16[128,1024]{1,0:T(8,128)(2,1)S(1)}, bf16[128,1024]{1,0:T(8,128)(2,1)}, u32[]{:S(2)}, u32[]{:S(2)}) collective-permute-start(bf16[128,1024]{1,0:T(8,128)(2,1)S(1)} %get-tuple-element.47), channel_id=1, source_target_pairs={{0,15},{1,0},{2,1},{3,2},{4,3},{5,4},{6,5},{7,6},{8,7},{9,8},{10,9... | collective-permute-start | bytes 786440 | tf_op jit(solution)/shard_map/ppermute | solution.py:22
  15.0 2.0 collective-permute-start.1
  17.0 0.3 fusion.16
  17.3 0.0 copy-start.5
  17.4 1.5 convolution_convert_fusion.3.ko.key1
  18.9 0.2 copy-done.5
  19.1 1.5 convolution_convert_fusion.2.vo.value1
  20.6 1.6 convolution_convert_fusion.9.ko
  22.2 1.5 convolution_convert_fusion.8.vo
  23.8 1.0 fusion.5.no
  24.7 1.5 convolution_convert_fusion.4.q.q1
  26.3 1.5 convolution_convert_fusion.10.q
  27.8 0.1 fusion.50
  27.9 0.1 pad_add_fusion
  28.0 0.1 copy.14
  28.1 0.2 fusion.22
  28.3 0.1 copy.15
  28.4 0.1 broadcast_bitcast_fusion
  28.4 3.2 %convolution_convert_fusion.5.ga = bf16[256,1024]{1,0:T(8,128)(2,1)} fusion(bf16[1,1024,1024]{2,1,0:T(8,128)(2,1)} %param.14, bf16[1,256,1024]{2,1,0:T(8,128)(2,1)S(1)} %copy-done.14), kind=kOutput, calls=%fused_computation.22 | convolution fusion | flops 537133056 | bytes 3145728 | tf_op jit(solution)/shard_map/dot_general | solution.py:32
  31.6 0.6 compare_select_fusion.mask
  32.2 1.0 fusion.17.no
  33.2 0.6 collective-permute-done
  33.7 0.2 fusion.14
  33.9 0.0 copy-start.3
  33.9 0.2 fusion.15.nh
  34.1 1.5 convolution_convert_fusion.6.vh
  35.6 0.1 copy-done.3
  35.7 1.6 convolution_convert_fusion.7.kh
  37.3 14.6 %attention_both_ways.1 = (bf16[1024,256]{1,0:T(8,128)(2,1)}, bf16[1024,256]{1,0:T(8,128)(2,1)}, bf16[1024,256]{1,0:T(8,128)(2,1)}, bf16[256,1024]{1,0:T(8,128)(2...) custom-call(bf16[256,1024]{1,0:T(8,128)(2,1)} %convolution_convert_f, ...), custom_call_target="tpu_custom_call" | custom-call | flops 1207959552 | bytes 6291456 | tf_op jit(solution)/shard_map/attention_both_ways/pallas_call | solution.py:160
  51.9 0.0 copy-start.7
  51.9 2.6 %fusion.33 = f32[256,1024]{1,0:T(8,128)S(1)} fusion(bf16[256,1024]{1,0:T(8,128)(2,1)} %get-tuple-element.22.kh0, bf16[1,1024,1024]{2,1,0:T(8,128)(2,1)} %param.12), kind=kOutput, calls=%fused_computation.76 | convolution fusion | flops 536870912 | bytes 3670016 | tf_op jit(solution)/shard_map/dot_general | solution.py:32
  54.6 0.7 fusion.6
  55.4 1.1 pad_maximum_fusion.1
  56.4 0.2 fusion.18
  56.6 0.0 copy-start.4
  56.6 0.2 fusion.19.nh
  56.8 1.5 convolution_convert_fusion.vh.value_halo1
  58.3 0.1 copy-done.4
  58.4 1.5 convolution_convert_fusion.1.kh.key_halo1
  59.9 0.8 fusion.48
  60.8 2.4 %collective-permute-start.5 = (bf16[128,1024]{1,0:T(8,128)(2,1)}, bf16[128,1024]{1,0:T(8,128)(2,1)S(1)}, u32[]{:S(2)}, u32[]{:S(2)}) collective-permute-start(bf16[128,1024]{1,0:T(8,128)(2,1)} %get-tuple-element.51), channel_id=1, source_target_pairs={{0,1},{1,2},{2,3},{3,4},{4,5},{5,6},{6,7},{7,8},{8,9},{9,10},{10,1... | collective-permute-start | bytes 786440 | tf_op jit(solution)/shard_map/ppermute | solution.py:22
  63.2 4.0 %collective-permute-start.4 = (bf16[128,1024]{1,0:T(8,128)(2,1)}, bf16[128,1024]{1,0:T(8,128)(2,1)}, u32[]{:S(2)}, u32[]{:S(2)}) collective-permute-start(bf16[128,1024]{1,0:T(8,128)(2,1)} %get-tuple-element.52), channel_id=1, source_target_pairs={{0,15},{1,0},{2,1},{3,2},{4,3},{5,4},{6,5},{7,6},{8,7},{9,8},{10,9... | collective-permute-start | bytes 786440 | tf_op jit(solution)/shard_map/ppermute | solution.py:22
  67.2 0.7 fusion.38
  67.9 9.3 %attention_forward.1 = (bf16[1024,256]{1,0:T(8,128)(2,1)}, bf16[1024,256]{1,0:T(8,128)(2,1)}, bf16[1024,256]{1,0:T(8,128)(2,1)}) custom-call(bf16[256,1024]{1,0:T(8,128)(2,1)} %convolution_convert_fusion.4.q.q1, bf16[256,1024]{1,0:T(8,128)(2,1)} %convolution_convert_fusion.3.ko.key1, bf16[256,1024]{1,0:T(8,128)(2,1)} %convolution_convert_fusion.2.vo.value1, ...), custom_call_target="tpu_custom_call" | custom-call | flops 402653184 | bytes 6291456 | tf_op jit(solution)/shard_map/attention_forward/pallas_call | solution.py:160
  77.2 0.0 copy-start.8
  77.2 2.5 %convolution_add_fusion.1 = f32[256,1024]{1,0:T(8,128)S(1)} fusion(f32[256,1024]{1,0:T(8,128)S(1)} %fusion.38, bf16[256,1024]{1,0:T(8,128)(2,1)S(1)} %copy-done.17, bf16[1,1024,1024]{2,1,0:T(8,128)(2,1)} %param.12), kind=kOutput, calls=%fused_computation.2 | convolution fusion | flops 537133056 | bytes 4718592 | tf_op jit(solution)/shard_map/dot_general | solution.py:32
  79.8 0.0 copy-start.15
  79.8 2.0 fusion.7
  81.8 0.0 copy-start.20
  81.9 0.3 fusion.11.grad_x0
  82.2 1.3 collective-permute-start.6
  83.5 2.5 %collective-permute-done.6 = bf16[256,1024]{1,0:T(8,128)(2,1)S(1)} collective-permute-done((bf16[256,1024]{1,0:T(8,128)(2,1)S(1)}, bf16[256,1024]{1,0:T(8,128)(2,1)S(1)}, u32[]{:S(2)}, u32[]{:S(2)}) %collective-permute-start.6) | collective-permute-done | bytes 524320 | tf_op jit(solution)/shard_map/ppermute | solution.py:28
  86.0 0.9 bitcast_select_fusion.up1
  86.9 120.3 %last_tick.1 = (f32[64,4,1024]{2,1,0:T(4,128)}, bf16[2,256,1024]{2,1,0:T(8,128)(2,1)}) custom-call(bf16[1024,256]{1,0:T(8,128)(2,1)} %get-tuple-element.20.n0, bf16[1024,256]{1,0:T(8,128)(2,1)} %get-tuple-element.21.nh0, bf16[1024,256]{1,0:T(8,128)(2,1)} %get-tuple-element.25.n1, bf16[1024,256]{1,0:T(8,128)(2,1)} %get-tuple-element.26.nh1, ...), custom_call_target="tpu_custom_call" | custom-call | flops 6442450944 | bytes 209715200 | tf_op jit(solution)/shard_map/last_tick/pallas_call | solution.py:381
  207.2 2.4 %copy.21 = f32[1,64,4,1024]{3,2,1,0:T(4,128)} copy(f32[1,64,4,1024]{3,2,1,0:T(4,128)} %bitcast.114) | data formatting | bytes 2097152
  209.6 1.0 copy.22
  (48 shorter events, 0.1 us)
Async XLA Ops:
  0.6 0.7 copy-start
  0.6 16.4 %copy-start.1 = (bf16[1,3,256,1024]{3,2,1,0:T(8,128)(2,1)S(1)}, bf16[1,3,256,1024]{3,2,1,0:T(8,128)(2,1)}, u32[]{:S(2)}) copy-start(bf16[1,3,256,1024]{3,2,1,0:T(8,128)(2,1)} %param.10) | copy-start | bytes 4718596
  5.8 11.6 %copy-start.2 = (bf16[1,1024,1024]{2,1,0:T(8,128)(2,1)S(1)}, bf16[1,1024,1024]{2,1,0:T(8,128)(2,1)}, u32[]{:S(2)}) copy-start(bf16[1,1024,1024]{2,1,0:T(8,128)(2,1)} %param.12) | copy-start | bytes 6291460
  8.1 47.3 %collective-permute-start.2 = (bf16[128,1024]{1,0:T(8,128)(2,1)}, bf16[128,1024]{1,0:T(8,128)(2,1)}, u32[]{:S(2)}, u32[]{:S(2)}) collective-permute-start(bf16[128,1024]{1,0:T(8,128)(2,1)} %get-tuple-element.46), channel_id=1, source_target_pairs={{0,1},{1,2},{2,3},{3,4},{4,5},{5,6},{6,7},{7,8},{8,9},{9,10},{10,1... | collective-permute-start | bytes 786440 | tf_op jit(solution)/shard_map/ppermute | solution.py:22
  11.0 44.4 %collective-permute-start.3 = (bf16[128,1024]{1,0:T(8,128)(2,1)S(1)}, bf16[128,1024]{1,0:T(8,128)(2,1)}, u32[]{:S(2)}, u32[]{:S(2)}) collective-permute-start(bf16[128,1024]{1,0:T(8,128)(2,1)S(1)} %get-tuple-element.47), channel_id=1, source_target_pairs={{0,15},{1,0},{2,1},{3,2},{4,3},{5,4},{6,5},{7,6},{8,7},{9,8},{10,9... | collective-permute-start | bytes 786440 | tf_op jit(solution)/shard_map/ppermute | solution.py:22
  15.0 18.2 %collective-permute-start.1 = (bf16[128,1024]{1,0:T(8,128)(2,1)}, bf16[128,1024]{1,0:T(8,128)(2,1)S(1)}, u32[]{:S(2)}, u32[]{:S(2)}) collective-permute-start(bf16[128,1024]{1,0:T(8,128)(2,1)} %get-tuple-element.48), channel_id=1, source_target_pairs={{0,15},{1,0},{2,1},{3,2},{4,3},{5,4},{6,5},{7,6},{8,7},{9,8},{10,9... | collective-permute-start | bytes 786440 | tf_op jit(solution)/shard_map/ppermute | solution.py:22
  17.0 16.7 %collective-permute-start = (bf16[128,1024]{1,0:T(8,128)(2,1)}, bf16[128,1024]{1,0:T(8,128)(2,1)S(1)}, u32[]{:S(2)}, u32[]{:S(2)}) collective-permute-start(bf16[128,1024]{1,0:T(8,128)(2,1)} %get-tuple-element.49), channel_id=1, source_target_pairs={{0,1},{1,2},{2,3},{3,4},{4,5},{5,6},{6,7},{7,8},{8,9},{9,10},{10,1... | collective-permute-start | bytes 786440 | tf_op jit(solution)/shard_map/ppermute | solution.py:22
  17.3 14.9 %copy-start.11 = (bf16[256,1024]{1,0:T(8,128)(2,1)}, bf16[256,1024]{1,0:T(8,128)(2,1)S(1)}, u32[]{:S(2)}) copy-start(bf16[256,1024]{1,0:T(8,128)(2,1)S(1)} %get-tuple-element.45.x1) | copy-start | bytes 1572868
  17.3 1.8 copy-start.5
  22.2 2.5 %copy-start.9 = (bf16[1,1024,1024]{2,1,0:T(8,128)(2,1)S(1)}, bf16[1,1024,1024]{2,1,0:T(8,128)(2,1)}, u32[]{:S(2)}) copy-start(bf16[1,1024,1024]{2,1,0:T(8,128)(2,1)} %param.11) | copy-start | bytes 6291460
  26.3 1.6 copy-start.23
  26.3 1.8 copy-start.24
  26.3 2.2 %copy-start.14 = (bf16[1,256,1024]{2,1,0:T(8,128)(2,1)S(1)}, bf16[1,256,1024]{2,1,0:T(8,128)(2,1)}, u32[]{:S(2)}) copy-start(bf16[1,256,1024]{2,1,0:T(8,128)(2,1)} %param.15) | copy-start | bytes 1572868
  31.6 2.5 %copy-start.6 = (bf16[1,1024,1024]{2,1,0:T(8,128)(2,1)S(1)}, bf16[1,1024,1024]{2,1,0:T(8,128)(2,1)}, u32[]{:S(2)}) copy-start(bf16[1,1024,1024]{2,1,0:T(8,128)(2,1)} %param.13) | copy-start | bytes 6291460
  33.9 1.8 copy-start.3
  34.1 3.2 %copy-start.19 = (bf16[256,1024]{1,0:T(8,128)(2,1)}, bf16[256,1024]{1,0:T(8,128)(2,1)S(1)}, u32[]{:S(2)}) copy-start(bf16[256,1024]{1,0:T(8,128)(2,1)S(1)} %fusion.15.nh) | copy-start | bytes 1572868
  51.9 2.7 %copy-start.7 = (bf16[1,1024,1024]{2,1,0:T(8,128)(2,1)S(1)}, bf16[1,1024,1024]{2,1,0:T(8,128)(2,1)}, u32[]{:S(2)}) copy-start(bf16[1,1024,1024]{2,1,0:T(8,128)(2,1)} %param.13) | copy-start | bytes 6291460
  51.9 2.7 %copy-start.22 = (bf16[256,1024]{1,0:T(8,128)(2,1)S(1)}, bf16[256,1024]{1,0:T(8,128)(2,1)}, u32[]{:S(2)}) copy-start(bf16[256,1024]{1,0:T(8,128)(2,1)} %get-tuple-element.23.vh0) | copy-start | bytes 1572868
  56.6 1.8 copy-start.4
  56.8 3.1 %copy-start.12 = (bf16[256,1024]{1,0:T(8,128)(2,1)}, bf16[256,1024]{1,0:T(8,128)(2,1)S(1)}, u32[]{:S(2)}) copy-start(bf16[256,1024]{1,0:T(8,128)(2,1)S(1)} %fusion.19.nh) | copy-start | bytes 1572868
  58.4 8.7 %copy-start.10 = (bf16[1,1024,1024]{2,1,0:T(8,128)(2,1)S(1)}, bf16[1,1024,1024]{2,1,0:T(8,128)(2,1)}, u32[]{:S(2)}) copy-start(bf16[1,1024,1024]{2,1,0:T(8,128)(2,1)} %param.11) | copy-start | bytes 6291460
  58.4 8.7 %copy-start.16 = (bf16[256,1024]{1,0:T(8,128)(2,1)S(1)}, bf16[256,1024]{1,0:T(8,128)(2,1)}, u32[]{:S(2)}) copy-start(bf16[256,1024]{1,0:T(8,128)(2,1)} %get-tuple-element.31.gq0) | copy-start | bytes 1572868
  60.8 19.0 %collective-permute-start.5 = (bf16[128,1024]{1,0:T(8,128)(2,1)}, bf16[128,1024]{1,0:T(8,128)(2,1)S(1)}, u32[]{:S(2)}, u32[]{:S(2)}) collective-permute-start(bf16[128,1024]{1,0:T(8,128)(2,1)} %get-tuple-element.51), channel_id=1, source_target_pairs={{0,1},{1,2},{2,3},{3,4},{4,5},{5,6},{6,7},{7,8},{8,9},{9,10},{10,1... | collective-permute-start | bytes 786440 | tf_op jit(solution)/shard_map/ppermute | solution.py:22
  63.2 16.6 %collective-permute-start.4 = (bf16[128,1024]{1,0:T(8,128)(2,1)}, bf16[128,1024]{1,0:T(8,128)(2,1)}, u32[]{:S(2)}, u32[]{:S(2)}) collective-permute-start(bf16[128,1024]{1,0:T(8,128)(2,1)} %get-tuple-element.52), channel_id=1, source_target_pairs={{0,15},{1,0},{2,1},{3,2},{4,3},{5,4},{6,5},{7,6},{8,7},{9,8},{10,9... | collective-permute-start | bytes 786440 | tf_op jit(solution)/shard_map/ppermute | solution.py:22
  67.9 9.3 %copy-start.17 = (bf16[256,1024]{1,0:T(8,128)(2,1)S(1)}, bf16[256,1024]{1,0:T(8,128)(2,1)}, u32[]{:S(2)}) copy-start(bf16[256,1024]{1,0:T(8,128)(2,1)} %get-tuple-element.32.ko0) | copy-start | bytes 1572868
  77.2 2.6 %copy-start.8 = (bf16[1,1024,1024]{2,1,0:T(8,128)(2,1)S(1)}, bf16[1,1024,1024]{2,1,0:T(8,128)(2,1)}, u32[]{:S(2)}) copy-start(bf16[1,1024,1024]{2,1,0:T(8,128)(2,1)} %param.13) | copy-start | bytes 6291460
  77.2 2.6 %copy-start.21 = (bf16[256,1024]{1,0:T(8,128)(2,1)S(1)}, bf16[256,1024]{1,0:T(8,128)(2,1)}, u32[]{:S(2)}) copy-start(bf16[256,1024]{1,0:T(8,128)(2,1)} %get-tuple-element.33.vo0) | copy-start | bytes 1572868
  79.8 2.0 copy-start.15
  81.8 4.2 %copy-start.20 = (bf16[1,256,1024]{2,1,0:T(8,128)(2,1)S(1)}, bf16[1,256,1024]{2,1,0:T(8,128)(2,1)}, u32[]{:S(2)}) copy-start(bf16[1,256,1024]{2,1,0:T(8,128)(2,1)} %param.16) | copy-start | bytes 1572868
  82.2 4.7 %copy-start.18 = (bf16[256,1024]{1,0:T(8,128)(2,1)}, bf16[256,1024]{1,0:T(8,128)(2,1)S(1)}, u32[]{:S(2)}) copy-start(bf16[256,1024]{1,0:T(8,128)(2,1)S(1)} %fusion.11.grad_x0) | copy-start | bytes 1572868
  82.2 3.8 %collective-permute-start.6 = (bf16[256,1024]{1,0:T(8,128)(2,1)S(1)}, bf16[256,1024]{1,0:T(8,128)(2,1)S(1)}, u32[]{:S(2)}, u32[]{:S(2)}) collective-permute-start(bf16[256,1024]{1,0:T(8,128)(2,1)S(1)} %fusion.11.grad_x0), channel_id=1, source_target_pairs={{16,0},{17,1},{18,2},{19,3},{20,4},{21,5},{22,6},{23,7},{24,8},{25... | collective-permute-start | bytes 1572872 | tf_op jit(solution)/shard_map/ppermute | solution.py:28
  207.2 2.4 %copy-start.13 = (bf16[2,256,1024]{2,1,0:T(8,128)(2,1)S(1)}, bf16[2,256,1024]{2,1,0:T(8,128)(2,1)}, u32[]{:S(2)}) copy-start(bf16[2,256,1024]{2,1,0:T(8,128)(2,1)} %get-tuple-element.37) | copy-start | bytes 3145732

commit v4 on v3

--- a/solution.py
+++ b/solution.py
@@ -51,9 +51,9 @@
 
 
 def softmax(q, k, mask, scale):
-    scores = right_dot(q, k) * scale + mask
-    raised = jnp.exp(scores - jnp.max(scores, axis=-1, keepdims=True))
-    return raised * (1.0 / jnp.sum(raised, axis=-1, keepdims=True))
+    scores = right_dot(k, q) * scale + mask
+    raised = jnp.exp(scores - jnp.max(scores, axis=0, keepdims=True))
+    return raised * (1.0 / jnp.sum(raised, axis=0, keepdims=True))
 
 
 def head_forward(scale, columns, q_ref, ko_ref, vo_ref, kh_ref, vh_ref, mask_ref, att_ref):
@@ -62,11 +62,10 @@
     for b in range(q_ref.shape[0] // BLOCK):
         rows = slice(b * BLOCK, (b + 1) * BLOCK)
         near = slice(b * BLOCK, (b + 3) * BLOCK)
-        probs = softmax(q_ref[rows, columns], keys[near], mask_ref[b : b + 1, :], scale)
-        att_ref[columns, rows] = lax.dot_general(
-            values[near], probs.astype(jnp.bfloat16), (((0,), (1,)), ((), ())),
-            preferred_element_type=jnp.float32,
-        ).astype(jnp.bfloat16)
+        probs = softmax(q_ref[rows, columns], keys[near], mask_ref[3 * b * BLOCK : 3 * (b + 1) * BLOCK, :], scale)
+        att_ref[columns, rows] = left_dot(values[near], probs.astype(jnp.bfloat16)).astype(
+            jnp.bfloat16
+        )
 
 
 def head_backward(
@@ -86,18 +85,16 @@
         ga = ga_ref[rows, columns]
         k = keys[near]
         v = values[near]
-        probs = softmax(q, k, mask_ref[b : b + 1, :], scale)
+        probs = softmax(q, k, mask_ref[3 * b * BLOCK : 3 * (b + 1) * BLOCK, :], scale)
         probs_bf = probs.astype(jnp.bfloat16)
         if att_ref is not None:
-            att_ref[columns, rows] = lax.dot_general(
-                v, probs_bf, (((0,), (1,)), ((), ())), preferred_element_type=jnp.float32
-            ).astype(jnp.bfloat16)
-        grad_probs = right_dot(ga, v)
-        inner = jnp.sum(probs * grad_probs, axis=-1, keepdims=True)
+            att_ref[columns, rows] = left_dot(v, probs_bf).astype(jnp.bfloat16)
+        grad_probs = right_dot(v, ga)
+        inner = jnp.sum(probs * grad_probs, axis=0, keepdims=True)
         scores_bf = (probs * (grad_probs - inner) * scale).astype(jnp.bfloat16)
-        gq_ref[rows, columns] = plain_dot(scores_bf, k).astype(jnp.bfloat16)
-        key_terms = left_dot(scores_bf, q)
-        value_terms = left_dot(probs_bf, ga)
+        gq_ref[rows, columns] = left_dot(scores_bf, k).astype(jnp.bfloat16)
+        key_terms = plain_dot(scores_bf, q)
+        value_terms = plain_dot(probs_bf, ga)
         for j in range(3):
             part = slice(j * size, (j + 1) * size)
             for sums, terms in ((key_sums, key_terms), (value_sums, value_terms)):
@@ -186,6 +183,7 @@
 )
 EARLY = 4
 LAG = 2
+AHEAD = 3
 
 
 def last_kernel(
@@ -331,7 +329,7 @@
         term_copy(side).start()
     for slot in (0, 1):
         arrange(nlhs, slot, orders[slot], (n0, n1, nh0, nh1))
-    for p in range(EARLY, len(PORTIONS)):
+    for p in range(EARLY, EARLY + AHEAD):
         begin(p)
     def finish_input():
         x_float = x1[...].astype(jnp.float32)
@@ -355,6 +353,8 @@
             advance(p, k)
     rest = range(EARLY, len(PORTIONS))
     for stage in range(len(rest) + LAG * (bits - 1)):
+        if stage + AHEAD < len(rest):
+            begin(rest[stage + AHEAD])
         for k in reversed(range(bits)):
             place = stage - LAG * k
             if 0 <= place < len(rest):
@@ -444,16 +444,17 @@
     inputs = [
         lax.dynamic_index_in_dim(saved_inputs[0], members[t], 0, keepdims=False) for t in (0, 1)
     ]
-    halos = [
-        jnp.concatenate(
+
+    def halo_of(x):
+        return jnp.concatenate(
             [
                 from_behind(x[rows_here - BLOCK :], "mesh", 1),
                 from_behind(x[:BLOCK], "mesh", -1),
             ],
             axis=0,
         )
-        for x in inputs
-    ]
+
+    halos = [halo_of(x) for x in inputs]
 
     positions = jnp.arange(BLOCK)
     block_ids = jnp.arange(counts.shape[0])
@@ -464,7 +465,9 @@
         axis=2,
     )
     mask = jnp.where(positions[None, None, :] < near_counts[:, :, None], 0.0, -jnp.inf)
-    mask = mask.reshape(blocks_here, 3 * BLOCK).astype(jnp.float32)
+    mask = jnp.broadcast_to(
+        mask.reshape(blocks_here * 3 * BLOCK, 1).astype(jnp.float32), (blocks_here * 3 * BLOCK, BLOCK)
+    )
 
     def ready(t):
         normed = norm(inputs[t])[2]

time: 211 us -> 199 us (0.943)
  Pallas kernels: 144 us -> 131 us
    pallas_call x2, Pallas kernels: 23.9 us -> 16.4 us  [attention(): pl.pallas_call(functools.partial(forward_kernel if ga is None else both_k...]
    pallas_call x1, Pallas kernels: 120 us -> 114 us  [last_tick(): pl.pallas_call(functools.partial(last_kernel, count), out_shape=[jax.Shap...]
    unnamed x53 -> x52, local copies, waits for them, and re-layouts: 4.51 us -> 4.43 us
  transfers between devices with their start and end apart: 7 -> 7, of which waited for: 2 -> 3; matrix products, arithmetic and copies ran while one was open for 12% -> 13% of each run, Pallas kernels for 11% -> 8%
where the time goes in v4:
time: 199 us; the launch traced here: 198 us
  Pallas kernels  131 us (66%)
  matrix products  27.2 us (14%)
  starting transfers between devices  16.6 us (8%)
  local copies, waits for them, and re-layouts  9.23 us (5%)
  other arithmetic  5.61 us (3%)
  between operations  4.85 us (2%)
  waiting for transfers between devices  3.95 us (2%)
    pallas_call x1, Pallas kernels, last_tick(): pl.pallas_call(functools.partial(last_kernel, count), out_shape=[jax.Shap...  114 us
    pallas_call x2, Pallas kernels, attention(): pl.pallas_call(functools.partial(forward_kernel if ga is None else both_k...  16.4 us
    dot_general x10, matrix products, plain_dot(): return jnp.dot(left, right, preferred_element_type=jnp.float32)  15.4 us
    ppermute x6, starting transfers between devices, from_behind(): return lax.ppermute(value, axis, pairs)  15.3 us
    dot_general x6, matrix products, right_dot(): lax.dot_general(left, right, (((1,), (1,)), ((), ())), preferred_element_...  11.8 us
    unnamed x52, local copies, waits for them, and re-layouts  4.43 us
  transfers between devices with their start and end apart: 7, of which 3 were waited for; matrix products, arithmetic and copies ran while one was open for 13% of the time, Pallas kernels for 8%

profile of v4, /device:TPU:0, one launch (start us, length us, event | category | flops | bytes accessed | tf_op | source)
XLA Modules:
  0.0 198.0 jit_solution(14286493607998195554)
XLA Ops:
  0.6 0.0 copy-start
  0.6 0.0 copy-start.1
  0.7 0.7 copy-done
  1.3 0.1 constant_dynamic-slice_fusion
  1.4 0.5 fusion.50
  5.8 0.0 copy-start.2
  5.8 2.3 %dynamic-slice_bitcast_fusion.2 = (bf16[128,1024]{1,0:T(8,128)(2,1)}, bf16[128,1024]{1,0:T(8,128)(2,1)S(1)}, bf16[128,1024]{1,0:T(8,128)(2,1)}, bf16[128,1024]{1,0:T(8,128)(2,1)}) fusion(bf16[1,3,256,1024]{3,2,1,0:T(8,128)(2,1)} %param.10, s32[]{:T(128)S(6)} %select_n.39, s32[]{:T(128)S(6)} %add.88, s32[]{:T(128)S(6)} %select_n.35), kind=kLoop, calls=%fused_computation.50 | loop fusion | bytes 2097164 | tf_op jit(solution)/shard_map/slice | solution.py:451
  8.1 2.9 %collective-permute-start.2 = (bf16[128,1024]{1,0:T(8,128)(2,1)}, bf16[128,1024]{1,0:T(8,128)(2,1)}, u32[]{:S(2)}, u32[]{:S(2)}) collective-permute-start(bf16[128,1024]{1,0:T(8,128)(2,1)} %get-tuple-element.46), channel_id=1, source_target_pairs={{0,1},{1,2},{2,3},{3,4},{4,5},{5,6},{6,7},{7,8},{8,9},{9,10},{10,1... | collective-permute-start | bytes 786440 | tf_op jit(solution)/shard_map/ppermute | solution.py:22
  11.0 4.0 %collective-permute-start.3 = (bf16[128,1024]{1,0:T(8,128)(2,1)S(1)}, bf16[128,1024]{1,0:T(8,128)(2,1)}, u32[]{:S(2)}, u32[]{:S(2)}) collective-permute-start(bf16[128,1024]{1,0:T(8,128)(2,1)S(1)} %get-tuple-element.47), channel_id=1, source_target_pairs={{0,15},{1,0},{2,1},{3,2},{4,3},{5,4},{6,5},{7,6},{8,7},{9,8},{10,9... | collective-permute-start | bytes 786440 | tf_op jit(solution)/shard_map/ppermute | solution.py:22
  15.0 2.0 %collective-permute-start.1 = (bf16[128,1024]{1,0:T(8,128)(2,1)}, bf16[128,1024]{1,0:T(8,128)(2,1)S(1)}, u32[]{:S(2)}, u32[]{:S(2)}) collective-permute-start(bf16[128,1024]{1,0:T(8,128)(2,1)} %get-tuple-element.48), channel_id=1, source_target_pairs={{0,15},{1,0},{2,1},{3,2},{4,3},{5,4},{6,5},{7,6},{8,7},{9,8},{10,9... | collective-permute-start | bytes 786440 | tf_op jit(solution)/shard_map/ppermute | solution.py:22
  17.0 0.3 fusion.16
  17.3 0.0 copy-start.5
  17.4 1.5 convolution_convert_fusion.3.ko.key1
  18.9 0.2 copy-done.5
  19.1 1.5 convolution_convert_fusion.2.vo.value1
  20.6 1.5 convolution_convert_fusion.9.ko
  22.2 1.5 convolution_convert_fusion.8.vo
  23.7 1.0 fusion.5.no
  24.7 1.5 convolution_convert_fusion.4.q.q1
  26.2 1.5 convolution_convert_fusion.10.q
  27.8 0.1 fusion.51
  27.9 0.1 pad_add_fusion
  27.9 0.1 copy.14
  28.0 0.2 fusion.23
  28.2 0.1 copy.15
  28.3 3.2 %convolution_convert_fusion.5.ga = bf16[256,1024]{1,0:T(8,128)(2,1)} fusion(bf16[1,1024,1024]{2,1,0:T(8,128)(2,1)} %param.14, bf16[1,256,1024]{2,1,0:T(8,128)(2,1)S(1)} %copy-done.15), kind=kOutput, calls=%fused_computation.22 | convolution fusion | flops 537133056 | bytes 3145728 | tf_op jit(solution)/shard_map/dot_general | solution.py:32
  31.5 0.1 fusion.22
  31.6 1.0 fusion.17.no
  32.5 1.2 collective-permute-done
  33.7 0.2 fusion.14
  33.9 0.0 copy-start.3
  33.9 0.2 fusion.15.nh
  34.1 1.5 convolution_convert_fusion.6.vh
  35.6 0.1 copy-done.3
  35.7 1.6 convolution_convert_fusion.7.kh
  37.3 0.9 broadcast_in_dim.46.mask
  38.2 10.5 %attention_both_ways.1 = (bf16[1024,256]{1,0:T(8,128)(2,1)}, bf16[1024,256]{1,0:T(8,128)(2,1)}, bf16[1024,256]{1,0:T(8,128)(2,1)}, bf16[256,1024]{1,0:T(8,128)(2...) custom-call(bf16[256,1024]{1,0:T(8,128)(2,1)} %convolution_convert_f, ...), custom_call_target="tpu_custom_call" | custom-call | flops 1207959552 | bytes 6291456 | tf_op jit(solution)/shard_map/attention_both_ways/pallas_call | solution.py:157
  48.7 0.0 copy-start.7
  48.7 2.6 %fusion.34 = f32[256,1024]{1,0:T(8,128)S(1)} fusion(bf16[256,1024]{1,0:T(8,128)(2,1)} %get-tuple-element.22.kh0, bf16[1,1024,1024]{2,1,0:T(8,128)(2,1)} %param.12), kind=kOutput, calls=%fused_computation.75 | convolution fusion | flops 536870912 | bytes 3670016 | tf_op jit(solution)/shard_map/dot_general | solution.py:32
  51.4 0.7 fusion.6
  52.1 1.1 pad_maximum_fusion.1
  53.2 0.2 fusion.18
  53.4 0.0 copy-start.4
  53.4 0.2 fusion.19.nh
  53.6 1.5 convolution_convert_fusion.vh.value_halo1
  55.1 0.1 copy-done.4
  55.2 1.5 convolution_convert_fusion.1.kh.key_halo1
  56.7 0.8 fusion.49
  57.5 2.4 %collective-permute-start.5 = (bf16[128,1024]{1,0:T(8,128)(2,1)}, bf16[128,1024]{1,0:T(8,128)(2,1)S(1)}, u32[]{:S(2)}, u32[]{:S(2)}) collective-permute-start(bf16[128,1024]{1,0:T(8,128)(2,1)} %get-tuple-element.51), channel_id=1, source_target_pairs={{0,1},{1,2},{2,3},{3,4},{4,5},{5,6},{6,7},{7,8},{8,9},{9,10},{10,1... | collective-permute-start | bytes 786440 | tf_op jit(solution)/shard_map/ppermute | solution.py:22
  59.9 4.0 %collective-permute-start.4 = (bf16[128,1024]{1,0:T(8,128)(2,1)}, bf16[128,1024]{1,0:T(8,128)(2,1)}, u32[]{:S(2)}, u32[]{:S(2)}) collective-permute-start(bf16[128,1024]{1,0:T(8,128)(2,1)} %get-tuple-element.52), channel_id=1, source_target_pairs={{0,15},{1,0},{2,1},{3,2},{4,3},{5,4},{6,5},{7,6},{8,7},{9,8},{10,9... | collective-permute-start | bytes 786440 | tf_op jit(solution)/shard_map/ppermute | solution.py:22
  63.9 0.7 fusion.39
  64.7 5.9 %attention_forward.1 = (bf16[1024,256]{1,0:T(8,128)(2,1)}, bf16[1024,256]{1,0:T(8,128)(2,1)}, bf16[1024,256]{1,0:T(8,128)(2,1)}) custom-call(bf16[256,1024]{1,0:T(8,128)(2,1)} %convolution_convert_fusion.4.q.q1, bf16[256,1024]{1,0:T(8,128)(2,1)} %convolution_convert_fusion.3.ko.key1, bf16[256,1024]{1,0:T(8,128)(2,1)} %convolution_convert_fusion.2.vo.value1, ...), custom_call_target="tpu_custom_call" | custom-call | flops 402653184 | bytes 6291456 | tf_op jit(solution)/shard_map/attention_forward/pallas_call | solution.py:157
  70.6 0.0 copy-start.8
  70.6 2.5 %convolution_add_fusion.1 = f32[256,1024]{1,0:T(8,128)S(1)} fusion(f32[256,1024]{1,0:T(8,128)S(1)} %fusion.39, bf16[256,1024]{1,0:T(8,128)(2,1)S(1)} %copy-done.18, bf16[1,1024,1024]{2,1,0:T(8,128)(2,1)} %param.12), kind=kOutput, calls=%fused_computation.2 | convolution fusion | flops 537133056 | bytes 4718592 | tf_op jit(solution)/shard_map/dot_general | solution.py:32
  73.1 0.3 collective-permute-done.4
  73.4 2.0 fusion.7
  75.4 0.0 copy-start.20
  75.4 0.3 fusion.11.grad_x0
  75.8 1.3 collective-permute-start.6
  77.1 2.5 %collective-permute-done.6 = bf16[256,1024]{1,0:T(8,128)(2,1)S(1)} collective-permute-done((bf16[256,1024]{1,0:T(8,128)(2,1)S(1)}, bf16[256,1024]{1,0:T(8,128)(2,1)S(1)}, u32[]{:S(2)}, u32[]{:S(2)}) %collective-permute-start.6) | collective-permute-done | bytes 524320 | tf_op jit(solution)/shard_map/ppermute | solution.py:28
  79.6 0.9 bitcast_select_fusion.up1
  80.5 114.2 %last_tick.1 = (f32[64,4,1024]{2,1,0:T(4,128)}, bf16[2,256,1024]{2,1,0:T(8,128)(2,1)}) custom-call(bf16[1024,256]{1,0:T(8,128)(2,1)} %get-tuple-element.20.n0, bf16[1024,256]{1,0:T(8,128)(2,1)} %get-tuple-element.21.nh0, bf16[1024,256]{1,0:T(8,128)(2,1)} %get-tuple-element.25.n1, bf16[1024,256]{1,0:T(8,128)(2,1)} %get-tuple-element.26.nh1, ...), custom_call_target="tpu_custom_call" | custom-call | flops 6442450944 | bytes 209715200 | tf_op jit(solution)/shard_map/last_tick/pallas_call | solution.py:381
  194.7 2.4 %copy.19 = f32[1,64,4,1024]{3,2,1,0:T(4,128)} copy(f32[1,64,4,1024]{3,2,1,0:T(4,128)} %bitcast.108) | data formatting | bytes 2097152
  197.0 1.0 copy.20
  (48 shorter events, 0.1 us)
Async XLA Ops:
  0.6 0.7 copy-start
  0.6 16.4 %copy-start.1 = (bf16[1,3,256,1024]{3,2,1,0:T(8,128)(2,1)S(1)}, bf16[1,3,256,1024]{3,2,1,0:T(8,128)(2,1)}, u32[]{:S(2)}) copy-start(bf16[1,3,256,1024]{3,2,1,0:T(8,128)(2,1)} %param.10) | copy-start | bytes 4718596
  5.8 11.6 %copy-start.2 = (bf16[1,1024,1024]{2,1,0:T(8,128)(2,1)S(1)}, bf16[1,1024,1024]{2,1,0:T(8,128)(2,1)}, u32[]{:S(2)}) copy-start(bf16[1,1024,1024]{2,1,0:T(8,128)(2,1)} %param.12) | copy-start | bytes 6291460
  8.1 44.1 %collective-permute-start.2 = (bf16[128,1024]{1,0:T(8,128)(2,1)}, bf16[128,1024]{1,0:T(8,128)(2,1)}, u32[]{:S(2)}, u32[]{:S(2)}) collective-permute-start(bf16[128,1024]{1,0:T(8,128)(2,1)} %get-tuple-element.46), channel_id=1, source_target_pairs={{0,1},{1,2},{2,3},{3,4},{4,5},{5,6},{6,7},{7,8},{8,9},{9,10},{10,1... | collective-permute-start | bytes 786440 | tf_op jit(solution)/shard_map/ppermute | solution.py:22
  11.0 41.1 %collective-permute-start.3 = (bf16[128,1024]{1,0:T(8,128)(2,1)S(1)}, bf16[128,1024]{1,0:T(8,128)(2,1)}, u32[]{:S(2)}, u32[]{:S(2)}) collective-permute-start(bf16[128,1024]{1,0:T(8,128)(2,1)S(1)} %get-tuple-element.47), channel_id=1, source_target_pairs={{0,15},{1,0},{2,1},{3,2},{4,3},{5,4},{6,5},{7,6},{8,7},{9,8},{10,9... | collective-permute-start | bytes 786440 | tf_op jit(solution)/shard_map/ppermute | solution.py:22
  15.0 17.6 %collective-permute-start.1 = (bf16[128,1024]{1,0:T(8,128)(2,1)}, bf16[128,1024]{1,0:T(8,128)(2,1)S(1)}, u32[]{:S(2)}, u32[]{:S(2)}) collective-permute-start(bf16[128,1024]{1,0:T(8,128)(2,1)} %get-tuple-element.48), channel_id=1, source_target_pairs={{0,15},{1,0},{2,1},{3,2},{4,3},{5,4},{6,5},{7,6},{8,7},{9,8},{10,9... | collective-permute-start | bytes 786440 | tf_op jit(solution)/shard_map/ppermute | solution.py:22
  17.0 16.7 %collective-permute-start = (bf16[128,1024]{1,0:T(8,128)(2,1)}, bf16[128,1024]{1,0:T(8,128)(2,1)S(1)}, u32[]{:S(2)}, u32[]{:S(2)}) collective-permute-start(bf16[128,1024]{1,0:T(8,128)(2,1)} %get-tuple-element.49), channel_id=1, source_target_pairs={{0,1},{1,2},{2,3},{3,4},{4,5},{5,6},{6,7},{7,8},{8,9},{9,10},{10,1... | collective-permute-start | bytes 786440 | tf_op jit(solution)/shard_map/ppermute | solution.py:22
  17.3 14.3 %copy-start.12 = (bf16[256,1024]{1,0:T(8,128)(2,1)}, bf16[256,1024]{1,0:T(8,128)(2,1)S(1)}, u32[]{:S(2)}) copy-start(bf16[256,1024]{1,0:T(8,128)(2,1)S(1)} %get-tuple-element.45.x1) | copy-start | bytes 1572868
  17.3 1.8 copy-start.5
  22.2 2.5 %copy-start.10 = (bf16[1,1024,1024]{2,1,0:T(8,128)(2,1)S(1)}, bf16[1,1024,1024]{2,1,0:T(8,128)(2,1)}, u32[]{:S(2)}) copy-start(bf16[1,1024,1024]{2,1,0:T(8,128)(2,1)} %param.11) | copy-start | bytes 6291460
  26.2 1.6 copy-start.23
  26.2 1.8 copy-start.24
  26.2 2.1 %copy-start.15 = (bf16[1,256,1024]{2,1,0:T(8,128)(2,1)S(1)}, bf16[1,256,1024]{2,1,0:T(8,128)(2,1)}, u32[]{:S(2)}) copy-start(bf16[1,256,1024]{2,1,0:T(8,128)(2,1)} %param.15) | copy-start | bytes 1572868
  31.6 2.5 %copy-start.6 = (bf16[1,1024,1024]{2,1,0:T(8,128)(2,1)S(1)}, bf16[1,1024,1024]{2,1,0:T(8,128)(2,1)}, u32[]{:S(2)}) copy-start(bf16[1,1024,1024]{2,1,0:T(8,128)(2,1)} %param.13) | copy-start | bytes 6291460
  33.9 1.8 copy-start.3
  34.1 3.2 %copy-start.9 = (bf16[256,1024]{1,0:T(8,128)(2,1)}, bf16[256,1024]{1,0:T(8,128)(2,1)S(1)}, u32[]{:S(2)}) copy-start(bf16[256,1024]{1,0:T(8,128)(2,1)S(1)} %fusion.15.nh) | copy-start | bytes 1572868
  48.7 2.7 %copy-start.7 = (bf16[1,1024,1024]{2,1,0:T(8,128)(2,1)S(1)}, bf16[1,1024,1024]{2,1,0:T(8,128)(2,1)}, u32[]{:S(2)}) copy-start(bf16[1,1024,1024]{2,1,0:T(8,128)(2,1)} %param.13) | copy-start | bytes 6291460
  48.7 2.7 %copy-start.22 = (bf16[256,1024]{1,0:T(8,128)(2,1)S(1)}, bf16[256,1024]{1,0:T(8,128)(2,1)}, u32[]{:S(2)}) copy-start(bf16[256,1024]{1,0:T(8,128)(2,1)} %get-tuple-element.23.vh0) | copy-start | bytes 1572868
  53.4 1.8 copy-start.4
  53.6 3.1 %copy-start.13 = (bf16[256,1024]{1,0:T(8,128)(2,1)}, bf16[256,1024]{1,0:T(8,128)(2,1)S(1)}, u32[]{:S(2)}) copy-start(bf16[256,1024]{1,0:T(8,128)(2,1)S(1)} %fusion.19.nh) | copy-start | bytes 1572868
  55.2 8.7 %copy-start.11 = (bf16[1,1024,1024]{2,1,0:T(8,128)(2,1)S(1)}, bf16[1,1024,1024]{2,1,0:T(8,128)(2,1)}, u32[]{:S(2)}) copy-start(bf16[1,1024,1024]{2,1,0:T(8,128)(2,1)} %param.11) | copy-start | bytes 6291460
  55.2 8.7 %copy-start.17 = (bf16[256,1024]{1,0:T(8,128)(2,1)S(1)}, bf16[256,1024]{1,0:T(8,128)(2,1)}, u32[]{:S(2)}) copy-start(bf16[256,1024]{1,0:T(8,128)(2,1)} %get-tuple-element.31.gq0) | copy-start | bytes 1572868
  57.5 15.6 %collective-permute-start.5 = (bf16[128,1024]{1,0:T(8,128)(2,1)}, bf16[128,1024]{1,0:T(8,128)(2,1)S(1)}, u32[]{:S(2)}, u32[]{:S(2)}) collective-permute-start(bf16[128,1024]{1,0:T(8,128)(2,1)} %get-tuple-element.51), channel_id=1, source_target_pairs={{0,1},{1,2},{2,3},{3,4},{4,5},{5,6},{6,7},{7,8},{8,9},{9,10},{10,1... | collective-permute-start | bytes 786440 | tf_op jit(solution)/shard_map/ppermute | solution.py:22
  59.9 13.5 %collective-permute-start.4 = (bf16[128,1024]{1,0:T(8,128)(2,1)}, bf16[128,1024]{1,0:T(8,128)(2,1)}, u32[]{:S(2)}, u32[]{:S(2)}) collective-permute-start(bf16[128,1024]{1,0:T(8,128)(2,1)} %get-tuple-element.52), channel_id=1, source_target_pairs={{0,15},{1,0},{2,1},{3,2},{4,3},{5,4},{6,5},{7,6},{8,7},{9,8},{10,9... | collective-permute-start | bytes 786440 | tf_op jit(solution)/shard_map/ppermute | solution.py:22
  64.7 5.9 %copy-start.18 = (bf16[256,1024]{1,0:T(8,128)(2,1)S(1)}, bf16[256,1024]{1,0:T(8,128)(2,1)}, u32[]{:S(2)}) copy-start(bf16[256,1024]{1,0:T(8,128)(2,1)} %get-tuple-element.32.ko0) | copy-start | bytes 1572868
  70.6 2.8 %copy-start.8 = (bf16[1,1024,1024]{2,1,0:T(8,128)(2,1)S(1)}, bf16[1,1024,1024]{2,1,0:T(8,128)(2,1)}, u32[]{:S(2)}) copy-start(bf16[1,1024,1024]{2,1,0:T(8,128)(2,1)} %param.13) | copy-start | bytes 6291460
  70.6 2.8 %copy-start.21 = (bf16[256,1024]{1,0:T(8,128)(2,1)S(1)}, bf16[256,1024]{1,0:T(8,128)(2,1)}, u32[]{:S(2)}) copy-start(bf16[256,1024]{1,0:T(8,128)(2,1)} %get-tuple-element.33.vo0) | copy-start | bytes 1572868
  73.4 2.0 %copy-start.16 = (bf16[1,256,1024]{2,1,0:T(8,128)(2,1)S(1)}, bf16[1,256,1024]{2,1,0:T(8,128)(2,1)}, u32[]{:S(2)}) copy-start(bf16[1,256,1024]{2,1,0:T(8,128)(2,1)} %param.15) | copy-start | bytes 1572868
  75.4 4.2 %copy-start.20 = (bf16[1,256,1024]{2,1,0:T(8,128)(2,1)S(1)}, bf16[1,256,1024]{2,1,0:T(8,128)(2,1)}, u32[]{:S(2)}) copy-start(bf16[1,256,1024]{2,1,0:T(8,128)(2,1)} %param.16) | copy-start | bytes 1572868
  75.8 4.7 %copy-start.19 = (bf16[256,1024]{1,0:T(8,128)(2,1)}, bf16[256,1024]{1,0:T(8,128)(2,1)S(1)}, u32[]{:S(2)}) copy-start(bf16[256,1024]{1,0:T(8,128)(2,1)S(1)} %fusion.11.grad_x0) | copy-start | bytes 1572868
  75.8 3.8 %collective-permute-start.6 = (bf16[256,1024]{1,0:T(8,128)(2,1)S(1)}, bf16[256,1024]{1,0:T(8,128)(2,1)S(1)}, u32[]{:S(2)}, u32[]{:S(2)}) collective-permute-start(bf16[256,1024]{1,0:T(8,128)(2,1)S(1)} %fusion.11.grad_x0), channel_id=1, source_target_pairs={{16,0},{17,1},{18,2},{19,3},{20,4},{21,5},{22,6},{23,7},{24,8},{25... | collective-permute-start | bytes 1572872 | tf_op jit(solution)/shard_map/ppermute | solution.py:28
  194.7 2.4 %copy-start.14 = (bf16[2,256,1024]{2,1,0:T(8,128)(2,1)S(1)}, bf16[2,256,1024]{2,1,0:T(8,128)(2,1)}, u32[]{:S(2)}) copy-start(bf16[2,256,1024]{2,1,0:T(8,128)(2,1)} %get-tuple-element.37) | copy-start | bytes 3145732
